TPU v7x, 128 devices: a whole 4x4x4 slice. The times are simulated.
128 devices in a mesh: dp: 8 (over z, core), mp: 16 (over y, x).
Axes of the slice: x: 4, y: 4, z: 4, core: 2. Of those that a mesh axis runs over, the one named last changes fastest.
Arguments:
- hidden: bfloat16 [4, 1024, 8192], P(None, 'dp'), may hold values from -6 to 6
- out_grads: bfloat16 [1024, 24576], P('dp', 'mp'), may hold values from -0.4375 to 0.4375
- mask_words: int32 [512, 24576], P(None, 'mp'), may hold values from 0 to 2925, as said below
- owner: int32 [16, 48], P('dp', 'mp'), may hold values from 0 to 15, as said below
- left_root: bfloat16 [1536, 512, 512], P(('dp', 'mp')), may hold values from -1 to 5, as said below
- right_root: bfloat16 [1536, 512, 512], P(('dp', 'mp')), may hold values from -1 to 5, as said below
Outputs:
- update: bfloat16 [8192, 24576], P('dp', 'mp')
Inputs may be any that keep to these rules, and one draw needn't show every extreme that they name: Each block's owner is an index along mp within the block's own dp row. A device hands at most 1 of its blocks to one owner, and some device does so in every dp row; every owner receives at least one block, none more than 12, and in every dp row one owner receives exactly 12. `mask_words`: every word holds four codes in base 8, each 0 to 5. `left_root`: symmetric matrices. `right_root`: symmetric matrices.
All inputs are finite; a program needn't handle non-finite values.
Results may differ from a plain program's by a relative error of at most 0.02.
Values may be sent and summed in bfloat16 or wider, within the bound.
A program may use at most 256 MiB of HBM per device.

v0:
```python
import jax
import jax.numpy as jnp
from jax import lax
from jax.sharding import PartitionSpec as P

D = 6144
FF = 8192
BLOCK = 512


def decode_codes(mask_words):
    powers = 8 ** jnp.arange(4, dtype=jnp.int32)
    group_codes = mask_words[:, None, :] // powers[None, :, None] % 8
    return group_codes.reshape(mask_words.shape[0] * 4, mask_words.shape[1])


def kept_selectors(group_codes):
    first_kept = jnp.where(group_codes >= 3, jnp.where(group_codes >= 5, 2, 1), 0)
    second_kept = jnp.where(
        group_codes == 0, 1, jnp.where((group_codes == 1) | (group_codes == 3), 2, 3)
    )
    lane_index = jnp.arange(4, dtype=jnp.int32)[None, :, None]
    select_first = (lane_index == first_kept[:, None, :]).astype(jnp.float32)
    select_second = (lane_index == second_kept[:, None, :]).astype(jnp.float32)
    return (select_first, select_second)


def pack_rows(dense_rows, group_codes):
    select_first, select_second = kept_selectors(group_codes)
    grouped = dense_rows.reshape(group_codes.shape[0], 4, dense_rows.shape[1])
    kept_first = jnp.sum(grouped * select_first, axis=1)
    kept_second = jnp.sum(grouped * select_second, axis=1)
    return jnp.stack([kept_first, kept_second], axis=1).reshape(-1, dense_rows.shape[1])


def unpack_rows(packed_rows, group_codes):
    select_first, select_second = kept_selectors(group_codes)
    paired = packed_rows.reshape(group_codes.shape[0], 2, packed_rows.shape[1])
    dense_rows = paired[:, 0:1, :] * select_first + paired[:, 1:2, :] * select_second
    return dense_rows.reshape(-1, packed_rows.shape[1])


def precondition(grad_blocks, left_blocks, right_blocks):
    right_applied = jnp.einsum(
        "kab,kbc->kac", grad_blocks, right_blocks, preferred_element_type=jnp.float32
    ).astype(jnp.bfloat16)
    preconditioned = jnp.einsum(
        "kab,kbc->kac", left_blocks, right_applied, preferred_element_type=jnp.float32
    )
    grad_float = grad_blocks.astype(jnp.float32)
    numerator = jnp.sqrt(jnp.mean(grad_float * grad_float, axis=(1, 2)))
    denominator = jnp.sqrt(jnp.mean(preconditioned * preconditioned, axis=(1, 2)) + 1e-06)
    return (preconditioned * (numerator / denominator)[:, None, None]).astype(jnp.bfloat16)


def body(hidden, out_grads, mask_words, owner, left_root, right_root):
    column_count = out_grads.shape[1]
    expert_index = lax.axis_index("mp") * column_count // D
    activations = lax.dynamic_index_in_dim(hidden, expert_index, 0, keepdims=False)
    group_codes = decode_codes(mask_words)
    replicas = lax.axis_size("dp")
    packed_count = FF // 2 // replicas
    own_codes = lax.dynamic_slice_in_dim(
        group_codes, lax.axis_index("dp") * (packed_count // 2), packed_count // 2, 0
    )
    dense_rows = lax.dot_general(
        activations, out_grads, (((0,), (0,)), ((), ())), preferred_element_type=jnp.float32
    )
    summed = lax.psum_scatter(
        pack_rows(dense_rows, group_codes).astype(jnp.bfloat16),
        "dp",
        scatter_dimension=0,
        tiled=True,
    ).astype(jnp.float32)
    gradient = unpack_rows(summed, own_codes).astype(jnp.bfloat16)
    row_blocks = gradient.shape[0] // BLOCK
    column_blocks = column_count // BLOCK
    grad_blocks = (
        gradient.reshape(row_blocks, BLOCK, column_blocks, BLOCK)
        .transpose(0, 2, 1, 3)
        .reshape(-1, BLOCK, BLOCK)
    )
    block_count = row_blocks * column_blocks
    targets = owner.reshape(-1)
    peer_count = lax.axis_size("mp")
    pair_slots = -(-block_count // peer_count)
    slot_total = peer_count * pair_slots
    same_owner = targets[:, None] == targets[None, :]
    block_order = jnp.arange(block_count, dtype=jnp.int32)
    earlier = block_order[None, :] < block_order[:, None]
    within = jnp.sum((same_owner & earlier).astype(jnp.int32), axis=1)
    send_slot = targets * pair_slots + within
    send_select = (jnp.arange(slot_total, dtype=jnp.int32)[:, None] == send_slot[None, :]).astype(
        jnp.bfloat16
    )
    owner_lists = lax.all_gather(targets.reshape(1, -1), "mp", axis=0, tiled=True)
    own_index = lax.axis_index("mp")
    arriving = jnp.sum((owner_lists == own_index).astype(jnp.int32), axis=1)
    present = (jnp.arange(pair_slots, dtype=jnp.int32)[None, :] < arriving[:, None]).reshape(-1)
    slot_ranks = jnp.cumsum(present.astype(jnp.int32)) - 1
    capacity = left_root.shape[0]
    gather_select = (
        (jnp.arange(capacity, dtype=jnp.int32)[:, None] == slot_ranks[None, :]) & present[None, :]
    ).astype(jnp.bfloat16)
    outgoing = jnp.einsum(
        "pj,jab->pab", send_select, grad_blocks, preferred_element_type=jnp.float32
    ).astype(jnp.bfloat16)
    arrived = lax.all_to_all(outgoing, "mp", split_axis=0, concat_axis=0, tiled=True)
    owned_blocks = jnp.einsum(
        "kp,pab->kab", gather_select, arrived, preferred_element_type=jnp.float32
    ).astype(jnp.bfloat16)
    scaled = precondition(owned_blocks, left_root, right_root)
    going_back = jnp.einsum(
        "kp,kab->pab", gather_select, scaled, preferred_element_type=jnp.float32
    ).astype(jnp.bfloat16)
    returned = lax.all_to_all(going_back, "mp", split_axis=0, concat_axis=0, tiled=True)
    updates = jnp.einsum(
        "pj,pab->jab", send_select, returned, preferred_element_type=jnp.float32
    ).astype(jnp.bfloat16)
    dense_update = (
        updates.reshape(row_blocks, column_blocks, BLOCK, BLOCK)
        .transpose(0, 2, 1, 3)
        .reshape(gradient.shape)
    )
    select_first, select_second = kept_selectors(own_codes)
    kept_mask = (select_first + select_second).reshape(gradient.shape)
    return (dense_update.astype(jnp.float32) * kept_mask).astype(jnp.bfloat16)


def solution(mesh):
    in_specs = (
        P(None, "dp", None),
        P("dp", "mp"),
        P(None, "mp"),
        P("dp", "mp"),
        P(("dp", "mp"), None, None),
        P(("dp", "mp"), None, None),
    )
    out_specs = P("dp", "mp")
    return jax.shard_map(body, mesh=mesh, in_specs=in_specs, out_specs=out_specs, check_vma=False)
```

profile of v0, /device:TPU:0, one launch (start us, length us, event | category | flops | bytes accessed | tf_op | source)
XLA Modules:
  0.0 876.8 jit_solution(16300450736338795833)
XLA Ops:
  24.0 14.9 %ne.168 = s32[2048,1536]{1,0:T(8,128)} reshape(s32[512,4,1536]{2,1,0:T(4,128)} %ne.167) | data formatting | bytes 25165824 | tf_op jit(solution)/shard_map/jit(floor_divide)/ne | solution.py:13
  44.9 15.0 %rem.68 = s32[2048,1536]{1,0:T(8,128)} reshape(s32[512,4,1536]{2,1,0:T(4,128)} %rem.67) | data formatting | bytes 25165824 | tf_op jit(solution)/shard_map/jit(floor_divide)/rem | solution.py:13
  59.9 135.6 %select_select_fusion = (s32[2048,1536]{1,0:T(8,128)}, s32[2048,1536]{1,0:T(8,128)}) fusion(s32[2048,1536]{1,0:T(8,128)} %rem.68, s32[2048]{0:T(1024)S(1)} %rem.70, s32[2048,1536]{1,0:T(8,128)} %ne.168, s32[2048]{0:T(1024)S(1)} %ne.176), kind=kLoop, calls=%fused_computation.13 | loop fusion | flops 75497472 | bytes 50348032 | tf_op jit(solution)/shard_map/jit(_where)/select_n | solution.py:19
  195.5 10.8 %select_select_fusion.1 = s32[2048,1536]{1,0:T(8,128)} fusion(s32[2048,1536]{1,0:T(8,128)} %get-tuple-element.8), kind=kLoop, calls=%fused_computation.14 | loop fusion | flops 12582912 | bytes 25165824 | tf_op jit(solution)/shard_map/jit(_where)/select_n | solution.py:18
  206.3 25.7 %select_reduce_fusion.1 = (bf16[2048,1536]{1,0:T(8,128)(2,1)}, bf16[2048,1536]{1,0:T(8,128)(2,1)}) fusion(s32[2048,1536]{1,0:T(8,128)} %select_select_fusion.1, s32[2048,1536]{1,0:T(8,128)} %get-tuple-element.7, bf16[128,1536]{1,0:T(8,128)(2,1)S(1)} %copy-done, bf16[2048,4,128]{2,1,0:T(4,128)(2,1)S(1)} %bitcast.60), kind=kOutput, calls=%fused_computation.2 | convolution fusion | flops 3290431488 | bytes 40239104 | tf_op jit(solution)/shard_map/dot_general | solution.py:66
  238.2 69.3 %copy.55 = bf16[2048,2,1536]{2,1,0:T(2,128)(2,1)} copy(bf16[2048,2,1536]{2,0,1:T(8,128)(2,1)S(1)} %pad_maximum_fusion) | data formatting | bytes 25165824 | tf_op jit(solution)/shard_map/stack | solution.py:33
  307.5 26.0 %convert_element_type.87 = bf16[4096,1536]{1,0:T(8,128)(2,1)} reshape(bf16[2048,2,1536]{2,1,0:T(2,128)(2,1)} %copy.55) | data formatting | bytes 25165824 | tf_op jit(solution)/shard_map/convert_element_type | solution.py:70
  339.1 12.1 %eq.201 = s32[2,512,3,512]{3,2,1,0:T(4,128)} reshape(s32[256,4,1536]{2,1,0:T(4,128)} %eq.200) | data formatting | bytes 12582912 | tf_op jit(solution)/shard_map/eq | solution.py:23
  354.9 12.0 %eq.216 = s32[2,512,3,512]{3,2,1,0:T(4,128)} reshape(s32[256,4,1536]{2,1,0:T(4,128)} %eq.215) | data formatting | bytes 12582912 | tf_op jit(solution)/shard_map/eq | solution.py:24
  367.4 41.3 %reduce-scatter.2.cloned.1.call-done = bf16[512,1536]{1,0:T(8,128)(2,1)} async-done(((bf16[4096,1536]{1,0:T(8,128)(2,1)}), bf16[512,1536]{1,0:T(8,128)(2,1)}) %reduce-scatter.2.cloned.1.call-update) | async-done | bytes 1572880 | tf_op jit(solution)/shard_map/reduce_scatter | solution.py:69
  419.6 12.5 %mul.108 = f32[2,512,3,512]{3,2,1,0:T(4,128)} reshape(f32[256,4,1536]{2,1,0:T(4,128)} %mul.107) | data formatting | bytes 12582912 | tf_op jit(solution)/shard_map/mul | solution.py:39
  436.0 12.0 %mul.112 = f32[2,512,3,512]{3,2,1,0:T(4,128)} reshape(f32[256,4,1536]{2,1,0:T(4,128)} %mul.111) | data formatting | bytes 12582912 | tf_op jit(solution)/shard_map/mul | solution.py:39
  447.9 12.1 %fusion.15 = bf16[2,3,512,512]{3,1,2,0:T(4,128)(2,1)S(1)} fusion(f32[2,512,3,512]{3,2,1,0:T(4,128)} %mul.112, s32[2,512,3,512]{3,2,1,0:T(4,128)} %eq.216, f32[2,512,3,512]{3,2,1,0:T(4,128)} %mul.108, s32[2,512,3,512]{3,2,1,0:T(4,128)} %eq.201, s32[2,512]{1,0:T(2,128)S(1)} %eq.198), kind=kLoop, calls=%fused_computation.35 | loop fusion | flops 9437184 | bytes 28315648 | tf_op jit(solution)/shard_map/transpose | solution.py:80
  460.8 7.4 convolution_convert_fusion.1
  468.2 11.4 %copy.58 = bf16[16,512,512]{2,1,0:T(8,128)(2,1)} copy(bf16[16,512,512]{2,0,1:T(8,128)(2,1)} %convolution_convert_fusion.1) | data formatting | bytes 16777216 | tf_op jit(solution)/shard_map/convert_element_type | solution.py:107
  479.5 6.9 all-to-all-start
  486.5 134.1 %all-gather = s32[16,1,6]{2,1,0:T(1,128)S(1)} all-gather(s32[1,1,6]{2,1,0:T(1,128)S(1)} %reshape.296), channel_id=1, replica_groups=mesh['dp'=8,'mp'=16] {'mp'}, dimensions={0}, use_global_device_ids=true | all-gather | bytes 408 | tf_op jit(solution)/shard_map/all_gather | solution.py:96
  621.3 11.5 %multiply_reduce_fusion = (f32[12]{0:T(128)S(1)}, bf16[12,512,512]{2,0,1:T(8,128)(2,1)}) fusion(bf16[16,512,512]{2,1,0:T(8,128)(2,1)} %all-to-all-done, s32[16]{0:T(128)S(1)} %add_reduce_fusion, pred[16]{0:T(512)(128)(4,1)S(1)} %get-tuple-element.13), kind=kOutput, calls=%fused_computation.8 | convolution fusion | flops 113246576 | bytes 14680192 | tf_op jit(solution)/shard_map/kp,pab->kab/dot_general | solution.py:109
  632.8 15.0 %fusion.10 = bf16[12,512,512]{2,1,0:T(8,128)(2,1)} fusion(bf16[12,512,512]{2,1,0:T(8,128)(2,1)} %param.11, bf16[12,512,512]{2,0,1:T(8,128)(2,1)} %get-tuple-element.18), kind=kOutput, calls=%fused_computation.26 | convolution fusion | flops 3221225472 | bytes 18874368 | tf_op jit(solution)/shard_map/kab,kbc->kac/dot_general | solution.py:44
  647.8 12.8 %multiply_reduce_fusion.1 = (f32[12]{0:T(128)S(1)}, f32[12,512,512]{2,1,0:T(8,128)}) fusion(bf16[12,512,512]{2,1,0:T(8,128)(2,1)} %fusion.10, bf16[12,512,512]{2,1,0:T(8,128)(2,1)} %param.10), kind=kOutput, calls=%fused_computation.12 | convolution fusion | flops 3227516928 | bytes 25165872 | tf_op jit(solution)/shard_map/kab,kbc->kac/dot_general | solution.py:47
  660.6 9.4 %fusion.9 = bf16[12,512,512]{1,2,0:T(8,128)(2,1)} fusion(f32[12,512,512]{2,1,0:T(8,128)} %get-tuple-element.16, f32[12]{0:T(128)S(1)} %rsqrt_multiply_fusion), kind=kLoop, calls=%fused_computation.25 | loop fusion | flops 6291456 | bytes 18874416 | tf_op jit(solution)/shard_map/convert_element_type | solution.py:53
  670.0 14.4 %copy.63 = bf16[12,512,512]{2,0,1:T(8,128)(2,1)} copy(bf16[12,512,512]{1,2,0:T(8,128)(2,1)} %fusion.9) | data formatting | bytes 12582912 | tf_op jit(solution)/shard_map/convert_element_type | solution.py:53
  684.4 9.0 %convolution_convert_fusion = bf16[16,512,512]{2,0,1:T(8,128)(2,1)} fusion(bf16[12,512,512]{2,0,1:T(8,128)(2,1)} %copy.63, s32[16]{0:T(128)S(1)} %add_reduce_fusion, pred[16]{0:T(512)(128)(4,1)S(1)} %get-tuple-element.13), kind=kOutput, calls=%fused_computation.23 | convolution fusion | flops 104857984 | bytes 14680144 | tf_op jit(solution)/shard_map/kp,kab->pab/dot_general | solution.py:113
  693.4 11.3 %copy.64 = bf16[16,512,512]{2,1,0:T(8,128)(2,1)} copy(bf16[16,512,512]{2,0,1:T(8,128)(2,1)} %convolution_convert_fusion) | data formatting | bytes 16777216 | tf_op jit(solution)/shard_map/convert_element_type | solution.py:115
  709.9 7.7 eq.221
  717.6 7.7 eq.223
  731.9 6.6 copy.69
  738.6 85.6 %all-to-all-done.1 = bf16[16,512,512]{2,1,0:T(8,128)(2,1)} async-done(((bf16[16,512,512]{2,1,0:T(8,128)(2,1)}), bf16[16,512,512]{2,1,0:T(8,128)(2,1)}, u32[]{:S(2)}, u32[]{:S(2)}) %all-to-all-start.1) | async-done | bytes 8388640 | tf_op jit(solution)/shard_map/all_to_all | solution.py:116
  824.2 8.2 convert_convert_fusion
  838.6 10.5 %copy.67 = f32[2,512,3,512]{1,0,3,2:T(2,128)} copy(f32[2,512,3,512]{3,1,2,0:T(8,128)} %bitcast.54) | data formatting | bytes 12582912 | tf_op jit(solution)/shard_map/convert_element_type | solution.py:127
  849.1 7.2 copy.76
  856.3 8.8 %multiply_convert_fusion.1 = bf16[1024,1536]{0,1:T(8,128)(2,1)} fusion(f32[1024,1536]{0,1:T(8,128)} %bitcast.58, s32[1024,1536]{0,1:T(8,128)} %copy.69, s32[1024,1536]{0,1:T(8,128)S(1)} %bitcast.57, s32[1024]{0:T(1024)S(1)} %eq.219), kind=kLoop, calls=%fused_computation.28 | loop fusion | flops 11010048 | bytes 22024192 | tf_op jit(solution)/shard_map/convert_element_type | solution.py:127
  (59 shorter events, 78.3 us)
Async XLA Ops:
  6.5 199.8 %copy-start = (bf16[128,1536]{1,0:T(8,128)(2,1)S(1)}, bf16[128,1536]{1,0:T(8,128)(2,1)}, u32[]{:S(2)}) copy-start(bf16[128,1536]{1,0:T(8,128)(2,1)} %param.7) | copy-start | bytes 1179652
  6.5 11.0 %copy-start.2 = (s32[512,1536]{1,0:T(8,128)S(1)}, s32[512,1536]{1,0:T(8,128)}, u32[]{:S(2)}) copy-start(s32[512,1536]{1,0:T(8,128)} %param.8) | copy-start | bytes 9437188
  6.5 402.2 %reduce-scatter.2.cloned.1.call-start = ((), (), s32[]{:S(2)}) async-start(), calls=%async_computation.3 | async-start | bytes 14155776 | tf_op jit(solution)/shard_map/reduce_scatter | solution.py:69
  195.5 10.9 %copy-start.3 = (bf16[1,128,8192]{1,2,0:T(8,128)(2,1)S(1)}, bf16[1,128,8192]{1,2,0:T(8,128)(2,1)}, u32[]{:S(2)}) copy-start(bf16[1,128,8192]{1,2,0:T(8,128)(2,1)} %copy.53) | copy-start | bytes 6291460
  354.9 12.2 %copy-start.5 = (s32[2,3]{1,0:T(2,128)S(1)}, s32[2,3]{1,0:T(2,128)}, u32[]{:S(2)}) copy-start(s32[2,3]{1,0:T(2,128)} %param.9) | copy-start | bytes 76
  419.6 12.5 %copy-start.4 = (f32[256,1,1536]{2,1,0:T(1,128)S(1)}, f32[256,1,1536]{2,1,0:T(1,128)}, u32[]{:S(2)}) copy-start(f32[256,1,1536]{2,1,0:T(1,128)} %get-tuple-element.12) | copy-start | bytes 4718596
  479.5 141.7 %all-to-all-start = ((bf16[16,512,512]{2,1,0:T(8,128)(2,1)}), bf16[16,512,512]{2,1,0:T(8,128)(2,1)}, u32[]{:S(2)}, u32[]{:S(2)}) async-start(bf16[16,512,512]{2,1,0:T(8,128)(2,1)} %copy.58), calls=%async_computation.1 | async-start | bytes 16777216 | tf_op jit(solution)/shard_map/all_to_all | solution.py:108
  704.7 119.4 %all-to-all-start.1 = ((bf16[16,512,512]{2,1,0:T(8,128)(2,1)}), bf16[16,512,512]{2,1,0:T(8,128)(2,1)}, u32[]{:S(2)}, u32[]{:S(2)}) async-start(bf16[16,512,512]{2,1,0:T(8,128)(2,1)} %copy.64), calls=%async_computation.2 | async-start | bytes 16777216 | tf_op jit(solution)/shard_map/all_to_all | solution.py:116
  849.1 7.2 slice-start
  849.1 7.2 slice-start.1
  856.3 13.5 %copy-start.1 = (bf16[128,1536]{1,0:T(8,128)(2,1)S(1)}, bf16[128,1536]{1,0:T(8,128)(2,1)}, u32[]{:S(2)}) copy-start(bf16[128,1536]{1,0:T(8,128)(2,1)} %param.7) | copy-start | bytes 1179652
Sparse Core Ops, SparseCore 0:
  333.6 75.0 reduce-scatter.1
where the time goes:
time: 894 us; the launch traced here: 877 us
  local copies, waits for them, and re-layouts  314 us (35%)
  other arithmetic  186 us (21%)
  blocking collectives  134 us (15%)
  waiting for transfers between devices  127 us (14%)
  matrix products  89.7 us (10%)
  between operations  13.8 us (2%)
  starting transfers between devices  12 us (1%)
    select_n x1, other arithmetic, kept_selectors(): jnp.where(group_codes == 0, 1, jnp.where((group_codes == 1) | (group_code...  136 us
    all_gather x1, blocking collectives, body(): lax.all_gather(targets.reshape(1, -1), 'mp', axis=0, tiled=True)  134 us
    all_to_all x1, waiting for transfers between devices, body(): lax.all_to_all(going_back, 'mp', split_axis=0, concat_axis=0, tiled=True)  85.6 us
    another operation x1, local copies, waits for them, and re-layouts, pack_rows(): jnp.stack([kept_first, kept_second], axis=1)  69.3 us
    reduce_scatter x1, waiting for transfers between devices, body(): lax.psum_scatter(pack_rows(dense_rows, group_codes).astype(jnp.bfloat16),...  41.3 us
    eq x8, local copies, waits for them, and re-layouts, kept_selectors(): select_first = (lane_index == first_kept[:, None, :]).astype(jnp.float32)  30.3 us
    eq x4, local copies, waits for them, and re-layouts, kept_selectors(): select_second = (lane_index == second_kept[:, None, :]).astype(jnp.float32)  30.1 us
    convert_element_type x1, local copies, waits for them, and re-layouts, body(): pack_rows(dense_rows, group_codes).astype(jnp.bfloat16)  26 us
  transfers between devices with their start and end apart: 3, of which 2 were waited for; matrix products, arithmetic and copies ran while one was open for 7% of the time, Pallas kernels for 0%

commit v1 on v0

v1 whole, which is shorter than its diff:
```python
import functools

import jax
import jax.numpy as jnp
from jax import lax
from jax.experimental import pallas as pl
from jax.experimental.pallas import tpu as pltpu
from jax.sharding import PartitionSpec as P

BLOCK = 512
HALF = BLOCK // 2
LANES = 128
SIDE = 4
SLOT_ROWS = BLOCK * BLOCK // LANES + 16
MESH = pl.DeviceIdType.MESH

NEAR = [(1, 0), (0, 1), (3, 0), (0, 3)]
STRAIGHT = [(2, 0), (0, 2)]
DIAGONAL = [(1, 1), (3, 3), (1, 3), (3, 1)]
FAR = [(2, 2)]
RELAYED = [
    ((2, 1), (0, 1), (2, 0)),
    ((1, 2), (1, 0), (0, 2)),
    ((2, 3), (0, 3), (2, 0)),
    ((3, 2), (3, 0), (0, 2)),
]


def slot_of(displacement):
    return displacement[1] * SIDE + displacement[0]


def triangles():
    row = lax.broadcasted_iota(jnp.int32, (HALF, HALF), 0)
    column = lax.broadcasted_iota(jnp.int32, (HALF, HALF), 1)
    as_bf16 = lambda test: jnp.where(test, 1.0, 0.0).astype(jnp.bfloat16)
    return as_bf16(row >= column), as_bf16(row < column), as_bf16(row > column), as_bf16(row == column)


def exchange_kernel(
    tokens, rows, columns, dp_size, mp_size, capacity,
    targets_ref, left_hbm, right_hbm, hidden_hbm, grads_hbm,
    roots_out, hidden_out, grads_out,
    left, right, send_slots, relay_slots, lists, lists_smem, ranks,
    load_sem, list_send, list_recv, slot_send, slot_recv, hop_send, hop_recv,
    gather_send, gather_recv, own_sem,
):
    d, m = lax.axis_index("dp"), lax.axis_index("mp")
    x, y = lax.rem(m, SIDE), m // SIDE

    def at(displacement):
        return lax.rem(y + displacement[1], SIDE) * SIDE + lax.rem(x + displacement[0], SIDE)

    loads = [
        pltpu.make_async_copy(left_hbm, left, load_sem.at[0]),
        pltpu.make_async_copy(right_hbm, right, load_sem.at[1]),
    ]
    for load in loads:
        load.start()

    barrier = pltpu.get_barrier_semaphore()
    for step in range(1, mp_size):
        pl.semaphore_signal(barrier, inc=1, device_id=(d, lax.rem(m + step, mp_size)), device_id_type=MESH)
    for step in range(1, dp_size):
        pl.semaphore_signal(barrier, inc=1, device_id=(lax.rem(d + step, dp_size), m), device_id_type=MESH)
    pl.semaphore_wait(barrier, mp_size - 1 + dp_size - 1)

    list_copies = []
    for step in range(1, mp_size):
        copy = pltpu.make_async_remote_copy(
            src_ref=targets_ref, dst_ref=lists.at[m], send_sem=list_send.at[step], recv_sem=list_recv.at[step],
            device_id=(d, lax.rem(m + step, mp_size)), device_id_type=MESH,
        )
        copy.start()
        list_copies.append(copy)
    lists[m] = targets_ref[...]

    expert = m * columns // (columns * SIDE)
    gathers = []
    for step in range(1, dp_size):
        peer = lax.rem(d + step, dp_size)
        features = pl.ds(pl.multiple_of(peer * rows, rows), rows)
        for which, (source, sink) in enumerate((
            (hidden_hbm.at[expert, :, features], hidden_out.at[d]),
            (grads_hbm, grads_out.at[d]),
        )):
            copy = pltpu.make_async_remote_copy(
                src_ref=source, dst_ref=sink, send_sem=gather_send.at[which, step], recv_sem=gather_recv.at[which, step],
                device_id=(peer, m), device_id_type=MESH,
            )
            copy.start()
            gathers.append(copy)
    own_features = pl.ds(pl.multiple_of(d * rows, rows), rows)
    own_copies = [
        pltpu.make_async_copy(hidden_hbm.at[expert, :, own_features], hidden_out.at[d], own_sem.at[0]),
        pltpu.make_async_copy(grads_hbm, grads_out.at[d], own_sem.at[1]),
    ]
    for copy in own_copies:
        copy.start()

    for copy in list_copies:
        copy.wait()
    to_smem = pltpu.make_async_copy(lists, lists_smem, load_sem.at[2])
    to_smem.start()
    to_smem.wait()

    def rank_step(sender, taken):
        ranks[sender] = jnp.minimum(taken, capacity - 1)
        hit = jnp.int32(0)
        for j in range(6):
            hit = jnp.where(lists_smem[sender, 0, j] == m, jnp.int32(1), hit)
        return taken + hit

    lax.fori_loop(0, mp_size, rank_step, jnp.int32(0))
    for load in loads:
        load.wait()

    lower, upper, _, eye = triangles()

    def pack(displacement):
        slot = slot_of(displacement)
        rank = ranks[at(displacement)]
        place = lax.broadcasted_iota(jnp.int32, (16, LANES), 0)
        extra = jnp.zeros((16, LANES), jnp.float32)
        for q, root in enumerate((left, right)):
            a = root[rank, 0:HALF, 0:HALF]
            b = root[rank, 0:HALF, HALF:BLOCK]
            c = root[rank, HALF:BLOCK, HALF:BLOCK]
            mixed = a * lower + c * upper
            diagonal = jnp.sum((c * eye).astype(jnp.float32), axis=0, keepdims=True)
            base = q * 4 * HALF
            for half in range(2):
                lanes = slice(half * LANES, (half + 1) * LANES)
                send_slots[slot, base + half * HALF : base + (half + 1) * HALF, :] = b[:, lanes]
                send_slots[slot, base + (2 + half) * HALF : base + (3 + half) * HALF, :] = mixed[:, lanes]
                extra = jnp.where(place == 2 * q + half, diagonal[:, lanes], extra)
        send_slots[slot, SLOT_ROWS - 16 : SLOT_ROWS, :] = extra.astype(jnp.bfloat16)

    hops = []
    for k, (displacement, first, second) in enumerate(RELAYED):
        pack(displacement)
        copy = pltpu.make_async_remote_copy(
            src_ref=send_slots.at[slot_of(displacement)], dst_ref=relay_slots.at[k],
            send_sem=hop_send.at[k], recv_sem=hop_recv.at[k], device_id=(d, at(first)), device_id_type=MESH,
        )
        copy.start()
        hops.append(copy)
    sends = []
    for displacement in FAR + DIAGONAL + STRAIGHT + NEAR:
        pack(displacement)
        slot = slot_of(displacement)
        copy = pltpu.make_async_remote_copy(
            src_ref=send_slots.at[slot], dst_ref=roots_out.at[slot],
            send_sem=slot_send.at[slot], recv_sem=slot_recv.at[slot], device_id=(d, at(displacement)), device_id_type=MESH,
        )
        copy.start()
        sends.append(copy)
    pack((0, 0))
    own_slot = pltpu.make_async_copy(send_slots.at[0], roots_out.at[0], own_sem.at[2])
    own_slot.start()
    for k, (displacement, first, second) in enumerate(RELAYED):
        hops[k].wait_recv()
        slot = slot_of(displacement)
        copy = pltpu.make_async_remote_copy(
            src_ref=relay_slots.at[k], dst_ref=roots_out.at[slot],
            send_sem=slot_send.at[slot], recv_sem=slot_recv.at[slot], device_id=(d, at(second)), device_id_type=MESH,
        )
        copy.start()
        sends.append(copy)
    own_slot.wait()
    for copy in own_copies:
        copy.wait()
    for hop in hops:
        hop.wait_send()
    for copy in gathers + sends:
        copy.wait()


def unpack(slot, q, full):
    lower, upper, strict, eye = triangles()
    base = q * 4 * HALF
    b = jnp.concatenate([slot[base : base + HALF, :], slot[base + HALF : base + 2 * HALF, :]], axis=1)
    mixed = jnp.concatenate([slot[base + 2 * HALF : base + 3 * HALF, :], slot[base + 3 * HALF : base + 4 * HALF, :]], axis=1)
    extra = slot[SLOT_ROWS - 16 : SLOT_ROWS, :].astype(jnp.float32)
    diagonal = jnp.concatenate([extra[2 * q : 2 * q + 1, :], extra[2 * q + 1 : 2 * q + 2, :]], axis=1).astype(jnp.bfloat16)
    turned = mixed.T
    full[0:HALF, 0:HALF] = mixed * lower + turned * upper
    full[0:HALF, HALF:BLOCK] = b
    full[HALF:BLOCK, 0:HALF] = b.T
    full[HALF:BLOCK, HALF:BLOCK] = mixed * upper + turned * strict + eye * diagonal


KEPT_ROWS = sum(bits << (4 * code) for code, bits in enumerate((3, 5, 9, 6, 10, 12)))


def kept_rows(words):
    count, columns = words.shape
    spread = jnp.broadcast_to(words[:, None, :], (count, 16, columns)).reshape(count * 16, columns)
    row = lax.broadcasted_iota(jnp.int32, (count * 16, columns), 0)
    code = jnp.bitwise_and(lax.shift_right_logical(spread, jnp.bitwise_and(row, 15) // 4 * 3), 7)
    bits = lax.shift_right_logical(jnp.full_like(code, KEPT_ROWS), code * 4 + jnp.bitwise_and(row, 3))
    return jnp.bitwise_and(bits, 1) == 1


def block_kernel(places, slot_ref, hidden_ref, grads_ref, words_ref, out_ref, left, right):
    tokens = hidden_ref.shape[0] * hidden_ref.shape[1]
    gradient = lax.dot_general(
        hidden_ref[...].reshape(tokens, BLOCK), grads_ref[...].reshape(tokens, BLOCK),
        (((0,), (0,)), ((), ())), preferred_element_type=jnp.float32,
    )
    kept = kept_rows(words_ref[...])
    block = jnp.where(kept, gradient, 0.0).astype(jnp.bfloat16)
    unpack(slot_ref.at[0], 0, left)
    unpack(slot_ref.at[0], 1, right)
    right_applied = jnp.dot(block, right[...], preferred_element_type=jnp.float32).astype(jnp.bfloat16)
    preconditioned = jnp.dot(left[...], right_applied, preferred_element_type=jnp.float32)
    wide = block.astype(jnp.float32)
    count = BLOCK * BLOCK
    numerator = jnp.sqrt(jnp.sum(wide * wide) / count)
    denominator = jnp.sqrt(jnp.sum(preconditioned * preconditioned) / count + 1e-06)
    out_ref[...] = jnp.where(kept, preconditioned * (numerator / denominator), 0.0).astype(jnp.bfloat16)


def body(dp_size, mp_size, hidden, out_grads, mask_words, owner, left_root, right_root):
    tokens, columns = out_grads.shape
    rows = hidden.shape[2] // dp_size
    capacity = left_root.shape[0]
    d, m = lax.axis_index("dp"), lax.axis_index("mp")
    targets = owner.reshape(-1)
    block_count = targets.shape[0]
    tile = jnp.full((8, LANES), -1, jnp.int32).at[0, :block_count].set(targets)
    any_space = pl.BlockSpec(memory_space=pl.ANY)
    slots, all_hidden, all_grads = pl.pallas_call(
        functools.partial(exchange_kernel, tokens, rows, columns, dp_size, mp_size, capacity),
        out_shape=(
            jax.ShapeDtypeStruct((mp_size, SLOT_ROWS, LANES), jnp.bfloat16),
            jax.ShapeDtypeStruct((dp_size, tokens, rows), jnp.bfloat16),
            jax.ShapeDtypeStruct((dp_size, tokens, columns), jnp.bfloat16),
        ),
        in_specs=[pl.BlockSpec(memory_space=pltpu.VMEM)] + [any_space] * 4,
        out_specs=(any_space,) * 3,
        scratch_shapes=[
            pltpu.VMEM(left_root.shape, jnp.bfloat16),
            pltpu.VMEM(right_root.shape, jnp.bfloat16),
            pltpu.VMEM((mp_size, SLOT_ROWS, LANES), jnp.bfloat16),
            pltpu.VMEM((len(RELAYED), SLOT_ROWS, LANES), jnp.bfloat16),
            pltpu.VMEM((mp_size, 8, LANES), jnp.int32),
            pltpu.SMEM((mp_size, 8, LANES), jnp.int32),
            pltpu.SMEM((mp_size,), jnp.int32),
            pltpu.SemaphoreType.DMA((3,)),
            pltpu.SemaphoreType.DMA((mp_size,)),
            pltpu.SemaphoreType.DMA((mp_size,)),
            pltpu.SemaphoreType.DMA((mp_size,)),
            pltpu.SemaphoreType.DMA((mp_size,)),
            pltpu.SemaphoreType.DMA((len(RELAYED),)),
            pltpu.SemaphoreType.DMA((len(RELAYED),)),
            pltpu.SemaphoreType.DMA((2, dp_size)),
            pltpu.SemaphoreType.DMA((2, dp_size)),
            pltpu.SemaphoreType.DMA((3,)),
        ],
        compiler_params=pltpu.CompilerParams(
            collective_id=0, has_side_effects=True, vmem_limit_bytes=56 * 2**20
        ),
        name="exchange",
    )(tile, left_root, right_root, hidden, out_grads)

    away_x = (m % SIDE - targets % SIDE + SIDE) % SIDE
    away_y = (m // SIDE - targets // SIDE + SIDE) % SIDE
    places = jnp.concatenate([away_y * SIDE + away_x, d[None]]).astype(jnp.int32)
    across = columns // BLOCK
    return pl.pallas_call(
        block_kernel,
        out_shape=jax.ShapeDtypeStruct((rows, columns), jnp.bfloat16),
        grid_spec=pltpu.PrefetchScalarGridSpec(
            num_scalar_prefetch=1,
            grid=(block_count,),
            in_specs=[
                pl.BlockSpec((1, SLOT_ROWS, LANES), lambda j, places: (places[j], 0, 0)),
                pl.BlockSpec((dp_size, tokens, BLOCK), lambda j, places: (0, 0, j // across)),
                pl.BlockSpec((dp_size, tokens, BLOCK), lambda j, places: (0, 0, j % across)),
                pl.BlockSpec(
                    (BLOCK // 16, BLOCK),
                    lambda j, places: (places[block_count] * (rows // BLOCK) + j // across, j % across),
                ),
            ],
            out_specs=pl.BlockSpec((BLOCK, BLOCK), lambda j, places: (j // across, j % across)),
            scratch_shapes=[
                pltpu.VMEM((BLOCK, BLOCK), jnp.bfloat16),
                pltpu.VMEM((BLOCK, BLOCK), jnp.bfloat16),
            ],
        ),
        compiler_params=pltpu.CompilerParams(vmem_limit_bytes=48 * 2**20),
        name="precondition",
    )(places, slots, all_hidden, all_grads, mask_words)


def solution(mesh):
    in_specs = (
        P(None, "dp", None),
        P("dp", "mp"),
        P(None, "mp"),
        P("dp", "mp"),
        P(("dp", "mp"), None, None),
        P(("dp", "mp"), None, None),
    )
    return jax.shard_map(
        functools.partial(body, mesh.shape["dp"], mesh.shape["mp"]),
        mesh=mesh, in_specs=in_specs, out_specs=P("dp", "mp"), check_vma=False,
    )
```

time: 894 us -> 132 us (0.15); the launches traced: 877 us -> 132 us
  local copies, waits for them, and re-layouts: 314 us -> 5.59 us
  other arithmetic: 186 us -> 0.1 us
  blocking collectives: 134 us -> 0 us
  waiting for transfers between devices: 127 us -> 0 us
  Pallas kernels: 0 us -> 126 us
  matrix products: 89.7 us -> 0 us
  between operations: 13.8 us -> 0.02 us
  starting transfers between devices: 12 us -> 0 us
    select_n x4 -> x0, other arithmetic: 148 us -> none  [the longest x1 136 us: kept_selectors(): jnp.where(group_codes == 0, 1, jnp.where((group_codes == 1) | (group_code...]
    all_gather x1 -> x0, blocking collectives: 134 us -> none  [body(): lax.all_gather(targets.reshape(1, -1), 'mp', axis=0, tiled=True)]
    pallas_call x0 -> x2, Pallas kernels: none -> 126 us  [the longest x1 110 us: body(): pl.pallas_call(functools.partial(exchange_kernel, tokens, rows, columns,...]
    dot_general x7 -> x0, matrix products: 89.7 us -> none  [the longest x1 25.7 us: body(): lax.dot_general(activations, out_grads, (((0,), (0,)), ((), ())), preferr...]
    all_to_all x2 -> x0, waiting for transfers between devices: 85.6 us -> none  [the longest x1 85.6 us: body(): lax.all_to_all(going_back, 'mp', split_axis=0, concat_axis=0, tiled=True)]
    convert_element_type x8 -> x0, local copies, waits for them, and re-layouts: 84.5 us -> none  [the longest x1 26 us: body(): pack_rows(dense_rows, group_codes).astype(jnp.bfloat16)]
    another operation x1, local copies, waits for them, and re-layouts: 69.3 us -> 0.76 us  [pack_rows(): jnp.stack([kept_first, kept_second], axis=1)]
    eq x12 -> x0, local copies, waits for them, and re-layouts: 60.5 us -> none  [the longest x8 30.3 us: kept_selectors(): select_first = (lane_index == first_kept[:, None, :]).astype(jnp.float32)]
  transfers between devices with their start and end apart: 3 -> 0, of which waited for: 2 -> 0; matrix products, arithmetic and copies ran while one was open for 7% -> 0% of each run, Pallas kernels for 0% -> 0%
where the time goes in v1:
time: 132 us
  Pallas kernels  126 us (95%)
  local copies, waits for them, and re-layouts  5.59 us (4%)
    pallas_call x1, Pallas kernels, body(): pl.pallas_call(functools.partial(exchange_kernel, tokens, rows, columns,...  110 us
    pallas_call x1, Pallas kernels, body(): pl.pallas_call(block_kernel, out_shape=jax.ShapeDtypeStruct((rows, column...  16.1 us
    unnamed x4, local copies, waits for them, and re-layouts  3.47 us

profile of v1, /device:TPU:0, one launch (start us, length us, event | category | flops | bytes accessed | tf_op | source)
XLA Modules:
  0.0 132.1 jit_solution(6682435225709757245)
XLA Ops:
  0.0 0.8 reshape.36
  0.8 0.8 reshape.35
  1.5 0.1 pad_add_fusion.places
  1.6 0.6 scatter.4.targets_ref
  2.2 110.3 %exchange.1 = (bf16[16,2064,128]{2,1,0:T(8,128)(2,1)}, bf16[8,128,1024]{2,1,0:T(8,128)(2,1)}, bf16[8,128,1536]{2,1,0:T(8,128)(2,1)}) custom-call(s32[8,128]{1,0:T(8,128)} %scatter.4.targets_ref, bf16[12,512,512]{2,1,0:T(8,128)(2,1)} %left_hbm.1, bf16[12,512,512]{2,1,0:T(8,128)(2,1)} %right_hbm.1, bf16[4,128,8192]{2,1,0:T(8,128)(2,1)} %hidden_hbm.1, ...), custom_call_target="tpu_custom_call" | custom-call | tf_op jit(solution)/shard_map/exchange/pallas_call | solution.py:233
  112.5 0.0 copy-start
  112.5 1.9 %copy-done = bf16[8,128,1536]{2,1,0:T(8,128)(2,1)S(1)} copy-done((bf16[8,128,1536]{2,1,0:T(8,128)(2,1)S(1)}, bf16[8,128,1536]{2,1,0:T(8,128)(2,1)}, u32[]{:S(2)}) %copy-start) | copy-done | bytes 3145752
  114.4 0.0 copy-start.1
  114.4 1.6 %copy-done.1 = bf16[8,128,1024]{2,1,0:T(8,128)(2,1)S(1)} copy-done((bf16[8,128,1024]{2,1,0:T(8,128)(2,1)S(1)}, bf16[8,128,1024]{2,1,0:T(8,128)(2,1)}, u32[]{:S(2)}) %copy-start.1) | copy-done | bytes 2097176
  116.0 16.1 %precondition.1 = bf16[1024,1536]{1,0:T(8,128)(2,1)} custom-call(s32[7]{0:T(128)S(1)} %pad_add_fusion.places, bf16[16,2064,128]{2,1,0:T(8,128)(2,1)} %get-tuple-element.20.slot_ref, bf16[8,128,1024]{2,1,0:T(8,128)(2,1)S(1)} %copy-done.1, bf16[8,128,1536]{2,1,0:T(8,128)(2,1)S(1)} %copy-done, s32[512,1536]{1,0:T(8,128)} %words_ref.1), custom_call_target="tpu_custom_call" | custom-call | tf_op jit(solution)/shard_map/precondition/pallas_call | solution.py:271
  (1 shorter events, 0.0 us)
Async XLA Ops:
  112.5 1.9 %copy-start = (bf16[8,128,1536]{2,1,0:T(8,128)(2,1)S(1)}, bf16[8,128,1536]{2,1,0:T(8,128)(2,1)}, u32[]{:S(2)}) copy-start(bf16[8,128,1536]{2,1,0:T(8,128)(2,1)} %get-tuple-element.22.grads_ref) | copy-start | bytes 9437188
  114.4 1.6 %copy-start.1 = (bf16[8,128,1024]{2,1,0:T(8,128)(2,1)S(1)}, bf16[8,128,1024]{2,1,0:T(8,128)(2,1)}, u32[]{:S(2)}) copy-start(bf16[8,128,1024]{2,1,0:T(8,128)(2,1)} %get-tuple-element.21.hidden_ref) | copy-start | bytes 6291460

commit v2 on v0

v2 whole, which is shorter than its diff:
```python
import functools

import jax
import jax.numpy as jnp
from jax import lax
from jax.experimental import pallas as pl
from jax.experimental.pallas import tpu as pltpu
from jax.sharding import PartitionSpec as P

BLOCK = 512
HALF = BLOCK // 2
LANES = 128
SIDE = 4
SLOT_ROWS = BLOCK * BLOCK // LANES + 16
MESH = pl.DeviceIdType.MESH

NEAR = [(1, 0), (0, 1), (3, 0), (0, 3)]
STRAIGHT = [(2, 0), (0, 2)]
DIAGONAL = [(1, 1), (3, 3), (1, 3), (3, 1)]
FAR = [(2, 2)]
RELAYED = [
    ((2, 1), (0, 1), (2, 0)),
    ((1, 2), (1, 0), (0, 2)),
    ((2, 3), (0, 3), (2, 0)),
    ((3, 2), (3, 0), (0, 2)),
]
ORDER = [(0, 0)] + FAR + STRAIGHT + DIAGONAL + NEAR + [legs[0] for legs in RELAYED]
SLOT = {displacement: slot for slot, displacement in enumerate(ORDER)}

KEPT_ROWS = sum(bits << (4 * code) for code, bits in enumerate((3, 5, 9, 6, 10, 12)))


def kept_rows(words):
    count, columns = words.shape
    spread = jnp.broadcast_to(words[:, None, :], (count, 16, columns)).reshape(count * 16, columns)
    row = lax.broadcasted_iota(jnp.int32, (count * 16, columns), 0)
    code = jnp.bitwise_and(lax.shift_right_logical(spread, jnp.bitwise_and(row, 15) // 4 * 3), 7)
    bits = lax.shift_right_logical(jnp.full_like(code, KEPT_ROWS), code * 4 + jnp.bitwise_and(row, 3))
    return jnp.bitwise_and(bits, 1) == 1


def exchange_kernel(
    rows, columns, dp_size, mp_size,
    owner, left_hbm, right_hbm, hidden_hbm, grads_hbm, words_hbm,
    scaled_out,
    left, right, send_slots, relay_slots, slots, hidden, grads, words, blocks, kept, left_full, right_full, triangles,
    tile, lists, lists_smem, ranks, block_of_slot, norms,
    load_sem, list_send, list_recv, slot_send, slot_recv, hop_send, hop_recv, gather_send, gather_recv, out_sem,
):
    capacity = left.shape[0]
    down, across = owner.shape
    block_count = down * across
    d, m = lax.axis_index("dp"), lax.axis_index("mp")
    x, y = lax.rem(m, SIDE), m // SIDE

    def at(displacement):
        return lax.rem(y + displacement[1], SIDE) * SIDE + lax.rem(x + displacement[0], SIDE)

    expert = m * columns // (columns * SIDE)
    own_features = pl.ds(pl.multiple_of(d * rows, rows), rows)
    own_words = pl.ds(pl.multiple_of(d * (rows // 16), rows // 16), rows // 16)
    root_loads = [
        pltpu.make_async_copy(left_hbm, left, load_sem.at[0]),
        pltpu.make_async_copy(right_hbm, right, load_sem.at[1]),
    ]
    own_loads = [
        pltpu.make_async_copy(hidden_hbm.at[expert, :, own_features], hidden.at[d], load_sem.at[2]),
        pltpu.make_async_copy(grads_hbm, grads.at[d], load_sem.at[3]),
        pltpu.make_async_copy(words_hbm.at[own_words], words, load_sem.at[4]),
    ]
    for load in root_loads + own_loads:
        load.start()

    barrier = pltpu.get_barrier_semaphore()
    for step in range(1, mp_size):
        pl.semaphore_signal(barrier, inc=1, device_id=(d, lax.rem(m + step, mp_size)), device_id_type=MESH)
    for step in range(1, dp_size):
        pl.semaphore_signal(barrier, inc=1, device_id=(lax.rem(d + step, dp_size), m), device_id_type=MESH)

    targets = [owner[j // across, j % across] for j in range(block_count)]
    lane = lax.broadcasted_iota(jnp.int32, (8, LANES), 1)
    listed = jnp.full((8, LANES), -1, jnp.int32)
    for j in range(block_count):
        listed = jnp.where(lane == j, targets[j], listed)
    tile[...] = listed
    row = lax.broadcasted_iota(jnp.int32, (HALF, HALF), 0)
    column = lax.broadcasted_iota(jnp.int32, (HALF, HALF), 1)
    for k, test in enumerate((row >= column, row < column, row > column, row == column)):
        triangles[k] = jnp.where(test, 1.0, 0.0).astype(jnp.bfloat16)
    pl.semaphore_wait(barrier, mp_size - 1 + dp_size - 1)

    list_copies = []
    for step in range(1, mp_size):
        copy = pltpu.make_async_remote_copy(
            src_ref=tile, dst_ref=lists.at[m], send_sem=list_send.at[step], recv_sem=list_recv.at[step],
            device_id=(d, lax.rem(m + step, mp_size)), device_id_type=MESH,
        )
        copy.start()
        list_copies.append(copy)
    lists[m] = listed

    gathers = []
    for step in range(1, dp_size):
        peer = lax.rem(d + step, dp_size)
        features = pl.ds(pl.multiple_of(peer * rows, rows), rows)
        for which, (source, sink) in enumerate((
            (hidden_hbm.at[expert, :, features], hidden.at[d]),
            (grads_hbm, grads.at[d]),
        )):
            copy = pltpu.make_async_remote_copy(
                src_ref=source, dst_ref=sink, send_sem=gather_send.at[which, step], recv_sem=gather_recv.at[which, step],
                device_id=(peer, m), device_id_type=MESH,
            )
            copy.start()
            gathers.append(copy)

    for copy in list_copies:
        copy.wait()
    to_smem = pltpu.make_async_copy(lists, lists_smem, load_sem.at[5])
    to_smem.start()

    for slot, displacement in enumerate(ORDER):
        sender = at((SIDE - displacement[0], SIDE - displacement[1]))
        block = jnp.int32(0)
        for j in range(1, block_count):
            block = jnp.where(targets[j] == sender, jnp.int32(j), block)
        block_of_slot[slot] = block
    to_smem.wait()

    def rank_step(sender, taken):
        ranks[sender] = jnp.minimum(taken, capacity - 1)
        hit = jnp.int32(0)
        for j in range(block_count):
            hit = jnp.where(lists_smem[sender, 0, j] == m, jnp.int32(1), hit)
        return taken + hit

    lax.fori_loop(0, mp_size, rank_step, jnp.int32(0))
    for load in root_loads:
        load.wait()

    def pack(displacement):
        slot = SLOT[displacement]
        rank = ranks[at(displacement)]
        place = lax.broadcasted_iota(jnp.int32, (16, LANES), 0)
        extra = jnp.zeros((16, LANES), jnp.float32)
        for q, root in enumerate((left, right)):
            a = root[rank, 0:HALF, 0:HALF]
            b = root[rank, 0:HALF, HALF:BLOCK]
            c = root[rank, HALF:BLOCK, HALF:BLOCK]
            mixed = a * triangles[0] + c * triangles[1]
            diagonal = jnp.sum((c * triangles[3]).astype(jnp.float32), axis=0, keepdims=True)
            base = q * 4 * HALF
            for half in range(2):
                lanes = slice(half * LANES, (half + 1) * LANES)
                send_slots[slot, base + half * HALF : base + (half + 1) * HALF, :] = b[:, lanes]
                send_slots[slot, base + (2 + half) * HALF : base + (3 + half) * HALF, :] = mixed[:, lanes]
                extra = jnp.where(place == 2 * q + half, diagonal[:, lanes], extra)
        send_slots[slot, SLOT_ROWS - 16 : SLOT_ROWS, :] = extra.astype(jnp.bfloat16)

    hops = []
    for k, (displacement, first, second) in enumerate(RELAYED):
        pack(displacement)
        copy = pltpu.make_async_remote_copy(
            src_ref=send_slots.at[SLOT[displacement]], dst_ref=relay_slots.at[k],
            send_sem=hop_send.at[k], recv_sem=hop_recv.at[k], device_id=(d, at(first)), device_id_type=MESH,
        )
        copy.start()
        hops.append(copy)
    sends = []
    for displacement in FAR + DIAGONAL + STRAIGHT + NEAR:
        pack(displacement)
        slot = SLOT[displacement]
        copy = pltpu.make_async_remote_copy(
            src_ref=send_slots.at[slot], dst_ref=slots.at[slot],
            send_sem=slot_send.at[slot], recv_sem=slot_recv.at[slot], device_id=(d, at(displacement)), device_id_type=MESH,
        )
        copy.start()
        sends.append(copy)
    pack((0, 0))
    pltpu.make_async_copy(send_slots.at[0], slots.at[0], slot_recv.at[0]).start()
    for k, (displacement, first, second) in enumerate(RELAYED):
        hops[k].wait_recv()
        slot = SLOT[displacement]
        copy = pltpu.make_async_remote_copy(
            src_ref=relay_slots.at[k], dst_ref=slots.at[slot],
            send_sem=slot_send.at[slot], recv_sem=slot_recv.at[slot], device_id=(d, at(second)), device_id_type=MESH,
        )
        copy.start()
        sends.append(copy)

    for load in own_loads:
        load.wait()
    for copy in gathers:
        copy.wait()

    def gradient_step(j, carry):
        features = pl.ds(pl.multiple_of(j // across * BLOCK, BLOCK), BLOCK)
        places = pl.ds(pl.multiple_of(lax.rem(j, across) * BLOCK, BLOCK), BLOCK)
        gradient = lax.dot_general(
            hidden[:, :, features].reshape(-1, BLOCK), grads[:, :, places].reshape(-1, BLOCK),
            (((0,), (0,)), ((), ())), preferred_element_type=jnp.float32,
        )
        in_words = pl.ds(pl.multiple_of(j // across * (BLOCK // 16), BLOCK // 16), BLOCK // 16)
        keep = jnp.where(kept_rows(words[in_words, places]), 1.0, 0.0)
        kept[j] = keep.astype(jnp.bfloat16)
        block = (gradient * keep).astype(jnp.bfloat16)
        blocks[j] = block
        wide = block.astype(jnp.float32)
        norms[j] = jnp.sum(wide * wide)
        return carry

    lax.fori_loop(0, block_count, gradient_step, 0)

    def unpack(slot, q, full):
        base = q * 4 * HALF
        part = lambda k: slots[slot, base + k * HALF : base + (k + 1) * HALF, :]
        b = jnp.concatenate([part(0), part(1)], axis=1)
        mixed = jnp.concatenate([part(2), part(3)], axis=1)
        extra = slots[slot, SLOT_ROWS - 16 : SLOT_ROWS, :].astype(jnp.float32)
        diagonal = jnp.concatenate([extra[2 * q : 2 * q + 1, :], extra[2 * q + 1 : 2 * q + 2, :]], axis=1)
        turned = mixed.T
        full[0:HALF, 0:HALF] = mixed * triangles[0] + turned * triangles[1]
        full[0:HALF, HALF:BLOCK] = b
        full[HALF:BLOCK, 0:HALF] = b.T
        full[HALF:BLOCK, HALF:BLOCK] = (
            mixed * triangles[1] + turned * triangles[2] + triangles[3] * diagonal.astype(jnp.bfloat16)
        )

    def out_copy(slot):
        return pltpu.make_async_copy(slots.at[slot, pl.ds(0, 4 * BLOCK)], scaled_out.at[slot], out_sem.at[slot])

    def slot_step(slot, carry):
        pltpu.make_async_copy(send_slots.at[slot], slots.at[slot], slot_recv.at[slot]).wait()
        j = block_of_slot[slot]
        unpack(slot, 1, right_full)
        right_applied = jnp.dot(blocks[j], right_full[...], preferred_element_type=jnp.float32).astype(jnp.bfloat16)
        unpack(slot, 0, left_full)
        preconditioned = jnp.dot(left_full[...], right_applied, preferred_element_type=jnp.float32)
        count = BLOCK * BLOCK
        numerator = jnp.sqrt(norms[j] / count)
        denominator = jnp.sqrt(jnp.sum(preconditioned * preconditioned) / count + 1e-06)
        scaled = (preconditioned * (numerator / denominator)).astype(jnp.bfloat16) * kept[j]
        for k in range(BLOCK // LANES):
            slots[slot, k * BLOCK : (k + 1) * BLOCK, :] = scaled[:, k * LANES : (k + 1) * LANES]
        out_copy(slot).start()
        return carry

    lax.fori_loop(0, mp_size, slot_step, 0)
    for hop in hops:
        hop.wait_send()
    for send in sends:
        send.wait_send()
    for slot in range(mp_size):
        out_copy(slot).wait()


def place_kernel(owner, scaled, out, held, load_sem, store_sem):
    down, across = owner.shape
    m = lax.axis_index("mp")
    loads, stores = [], []
    for j in range(down * across):
        target = owner[j // across, j % across]
        away_x = lax.rem(lax.rem(m, SIDE) - lax.rem(target, SIDE) + SIDE, SIDE)
        away_y = lax.rem(m // SIDE - target // SIDE + SIDE, SIDE)
        slot = jnp.int32(0)
        for index, (dx, dy) in enumerate(ORDER):
            slot = jnp.where((away_x == dx) & (away_y == dy), jnp.int32(index), slot)
        rows = pl.ds(j // across * BLOCK, BLOCK)
        columns = pl.ds(j % across * BLOCK, BLOCK)
        loads.append([
            pltpu.make_async_copy(
                scaled.at[slot, pl.ds(k * BLOCK, BLOCK)], held.at[j, :, pl.ds(k * LANES, LANES)], load_sem.at[j, k]
            )
            for k in range(BLOCK // LANES)
        ])
        stores.append(pltpu.make_async_copy(held.at[j], out.at[rows, columns], store_sem.at[j]))
        for load in loads[-1]:
            load.start()
    for parts, store in zip(loads, stores):
        for load in parts:
            load.wait()
        store.start()
    for store in stores:
        store.wait()


def body(dp_size, mp_size, hidden, out_grads, mask_words, owner, left_root, right_root):
    tokens, columns = out_grads.shape
    rows = hidden.shape[2] // dp_size
    block_count = owner.size
    any_space = pl.BlockSpec(memory_space=pl.ANY)
    in_smem = pl.BlockSpec(memory_space=pltpu.SMEM)
    blocks = pltpu.VMEM((block_count, BLOCK, BLOCK), jnp.bfloat16)
    slots = pltpu.VMEM((mp_size, SLOT_ROWS, LANES), jnp.bfloat16)
    full = pltpu.VMEM((BLOCK, BLOCK), jnp.bfloat16)
    scaled = pl.pallas_call(
        functools.partial(exchange_kernel, rows, columns, dp_size, mp_size),
        out_shape=jax.ShapeDtypeStruct((mp_size, 4 * BLOCK, LANES), jnp.bfloat16),
        in_specs=[in_smem] + [any_space] * 5,
        out_specs=any_space,
        scratch_shapes=[
            pltpu.VMEM(left_root.shape, jnp.bfloat16),
            pltpu.VMEM(right_root.shape, jnp.bfloat16),
            slots,
            pltpu.VMEM((len(RELAYED), SLOT_ROWS, LANES), jnp.bfloat16),
            slots,
            pltpu.VMEM((dp_size, tokens, rows), jnp.bfloat16),
            pltpu.VMEM((dp_size, tokens, columns), jnp.bfloat16),
            pltpu.VMEM((rows // 16, columns), jnp.int32),
            blocks,
            blocks,
            full,
            full,
            pltpu.VMEM((4, HALF, HALF), jnp.bfloat16),
            pltpu.VMEM((8, LANES), jnp.int32),
            pltpu.VMEM((mp_size, 8, LANES), jnp.int32),
            pltpu.SMEM((mp_size, 8, LANES), jnp.int32),
            pltpu.SMEM((mp_size,), jnp.int32),
            pltpu.SMEM((mp_size,), jnp.int32),
            pltpu.SMEM((block_count,), jnp.float32),
            pltpu.SemaphoreType.DMA((6,)),
            pltpu.SemaphoreType.DMA((mp_size,)),
            pltpu.SemaphoreType.DMA((mp_size,)),
            pltpu.SemaphoreType.DMA((mp_size,)),
            pltpu.SemaphoreType.DMA((mp_size,)),
            pltpu.SemaphoreType.DMA((len(RELAYED),)),
            pltpu.SemaphoreType.DMA((len(RELAYED),)),
            pltpu.SemaphoreType.DMA((2, dp_size)),
            pltpu.SemaphoreType.DMA((2, dp_size)),
            pltpu.SemaphoreType.DMA((mp_size,)),
        ],
        compiler_params=pltpu.CompilerParams(
            collective_id=0, has_side_effects=True, vmem_limit_bytes=58 * 2**20
        ),
        name="exchange",
    )(owner, left_root, right_root, hidden, out_grads, mask_words)
    return pl.pallas_call(
        place_kernel,
        out_shape=jax.ShapeDtypeStruct((rows, columns), jnp.bfloat16),
        in_specs=[in_smem, any_space],
        out_specs=any_space,
        scratch_shapes=[
            blocks,
            pltpu.SemaphoreType.DMA((block_count, BLOCK // LANES)),
            pltpu.SemaphoreType.DMA((block_count,)),
        ],
        name="place",
    )(owner, scaled)


def solution(mesh):
    in_specs = (
        P(None, "dp", None),
        P("dp", "mp"),
        P(None, "mp"),
        P("dp", "mp"),
        P(("dp", "mp"), None, None),
        P(("dp", "mp"), None, None),
    )
    return jax.shard_map(
        functools.partial(body, mesh.shape["dp"], mesh.shape["mp"]),
        mesh=mesh, in_specs=in_specs, out_specs=P("dp", "mp"), check_vma=False,
    )
```

time: 894 us -> 118 us (0.13); the launches traced: 877 us -> 118 us
  local copies, waits for them, and re-layouts: 314 us -> 0 us
  other arithmetic: 186 us -> 0 us
  blocking collectives: 134 us -> 0 us
  waiting for transfers between devices: 127 us -> 0 us
  Pallas kernels: 0 us -> 118 us
  matrix products: 89.7 us -> 0 us
  between operations: 13.8 us -> 0.01 us
  starting transfers between devices: 12 us -> 0 us
    select_n x4 -> x0, other arithmetic: 148 us -> none  [the longest x1 136 us: kept_selectors(): jnp.where(group_codes == 0, 1, jnp.where((group_codes == 1) | (group_code...]
    all_gather x1 -> x0, blocking collectives: 134 us -> none  [body(): lax.all_gather(targets.reshape(1, -1), 'mp', axis=0, tiled=True)]
    pallas_call x0 -> x2, Pallas kernels: none -> 118 us  [the longest x1 114 us: body(): pl.pallas_call(functools.partial(exchange_kernel, rows, columns, dp_size,...]
    dot_general x7 -> x0, matrix products: 89.7 us -> none  [the longest x1 25.7 us: body(): lax.dot_general(activations, out_grads, (((0,), (0,)), ((), ())), preferr...]
    all_to_all x2 -> x0, waiting for transfers between devices: 85.6 us -> none  [the longest x1 85.6 us: body(): lax.all_to_all(going_back, 'mp', split_axis=0, concat_axis=0, tiled=True)]
    convert_element_type x8 -> x0, local copies, waits for them, and re-layouts: 84.5 us -> none  [the longest x1 26 us: body(): pack_rows(dense_rows, group_codes).astype(jnp.bfloat16)]
    another operation x1 -> x0, local copies, waits for them, and re-layouts: 69.3 us -> none  [pack_rows(): jnp.stack([kept_first, kept_second], axis=1)]
    eq x12 -> x0, local copies, waits for them, and re-layouts: 60.5 us -> none  [the longest x8 30.3 us: kept_selectors(): select_first = (lane_index == first_kept[:, None, :]).astype(jnp.float32)]
  transfers between devices with their start and end apart: 3 -> 0, of which waited for: 2 -> 0; matrix products, arithmetic and copies ran while one was open for 7% -> 0% of each run, Pallas kernels for 0% -> 0%
where the time goes in v2:
time: 118 us
  Pallas kernels  118 us (100%)
    pallas_call x1, Pallas kernels, body(): pl.pallas_call(functools.partial(exchange_kernel, rows, columns, dp_size,...  114 us
    pallas_call x1, Pallas kernels, body(): pl.pallas_call(place_kernel, out_shape=jax.ShapeDtypeStruct((rows, column...  3.76 us

profile of v2, /device:TPU:0, one launch (start us, length us, event | category | flops | bytes accessed | tf_op | source)
XLA Modules:
  0.0 117.8 jit_solution(899178476219300071)
XLA Ops:
  0.0 114.0 %exchange.1.scaled = bf16[16,2048,128]{2,1,0:T(8,128)(2,1)} custom-call(s32[2,3]{1,0:T(2,128)} %owner.3, bf16[12,512,512]{2,1,0:T(8,128)(2,1)} %left_hbm.1, bf16[12,512,512]{2,1,0:T(8,128)(2,1)} %right_hbm.1, bf16[4,128,8192]{2,1,0:T(8,128)(2,1)} %hidden_hbm.1, bf16[128,1536]{1,0:T(8,128)(2,1)} %grads_hbm.1, s32[512,1536]{1,0:T(8,128)} %words_hbm.1), custom_call_target="tpu_custom_call" | custom-call | tf_op jit(solution)/shard_map/exchange/pallas_call | solution.py:296
  114.0 3.8 %place.1 = bf16[1024,1536]{1,0:T(8,128)(2,1)} custom-call(s32[2,3]{1,0:T(2,128)} %owner.3, bf16[16,2048,128]{2,1,0:T(8,128)(2,1)} %exchange.1.scaled), custom_call_target="tpu_custom_call" | custom-call | tf_op jit(solution)/shard_map/place/pallas_call | solution.py:337

commit v3 on v2

--- a/solution.py
+++ b/solution.py
@@ -24,7 +24,8 @@
     ((2, 3), (0, 3), (2, 0)),
     ((3, 2), (3, 0), (0, 2)),
 ]
-ORDER = [(0, 0)] + FAR + STRAIGHT + DIAGONAL + NEAR + [legs[0] for legs in RELAYED]
+ORDER = [(0, 0)] + NEAR + STRAIGHT + DIAGONAL + FAR + [legs[0] for legs in RELAYED]
+DIRECT = len(ORDER) - len(RELAYED)
 SLOT = {displacement: slot for slot, displacement in enumerate(ORDER)}
 
 KEPT_ROWS = sum(bits << (4 * code) for code, bits in enumerate((3, 5, 9, 6, 10, 12)))
@@ -43,9 +44,9 @@
     rows, columns, dp_size, mp_size,
     owner, left_hbm, right_hbm, hidden_hbm, grads_hbm, words_hbm,
     scaled_out,
-    left, right, send_slots, relay_slots, slots, hidden, grads, words, blocks, kept, left_full, right_full, triangles,
+    left, right, send_slots, relay_slots, slots, hidden, grads, words, blocks, kept, left_full, right_full, triangles, halfway,
     tile, lists, lists_smem, ranks, block_of_slot, norms,
-    load_sem, list_send, list_recv, slot_send, slot_recv, hop_send, hop_recv, gather_send, gather_recv, out_sem,
+    load_sem, list_send, list_recv, slot_send, slot_recv, hop_send, hop_recv, last_send, last_recv, gather_send, gather_recv, out_sem,
 ):
     capacity = left.shape[0]
     down, across = owner.shape
@@ -78,8 +79,8 @@
         pl.semaphore_signal(barrier, inc=1, device_id=(lax.rem(d + step, dp_size), m), device_id_type=MESH)
 
     targets = [owner[j // across, j % across] for j in range(block_count)]
-    lane = lax.broadcasted_iota(jnp.int32, (8, LANES), 1)
-    listed = jnp.full((8, LANES), -1, jnp.int32)
+    lane = lax.broadcasted_iota(jnp.int32, (1, LANES), 1)
+    listed = jnp.full((1, LANES), -1, jnp.int32)
     for j in range(block_count):
         listed = jnp.where(lane == j, targets[j], listed)
     tile[...] = listed
@@ -89,14 +90,11 @@
         triangles[k] = jnp.where(test, 1.0, 0.0).astype(jnp.bfloat16)
     pl.semaphore_wait(barrier, mp_size - 1 + dp_size - 1)
 
-    list_copies = []
     for step in range(1, mp_size):
-        copy = pltpu.make_async_remote_copy(
-            src_ref=tile, dst_ref=lists.at[m], send_sem=list_send.at[step], recv_sem=list_recv.at[step],
+        pltpu.make_async_remote_copy(
+            src_ref=tile, dst_ref=lists.at[m], send_sem=list_send.at[0], recv_sem=list_recv.at[0],
             device_id=(d, lax.rem(m + step, mp_size)), device_id_type=MESH,
-        )
-        copy.start()
-        list_copies.append(copy)
+        ).start()
     lists[m] = listed
 
     gathers = []
@@ -114,8 +112,8 @@
             copy.start()
             gathers.append(copy)
 
-    for copy in list_copies:
-        copy.wait()
+    others = lists.at[pl.ds(0, mp_size - 1)]
+    pltpu.make_async_copy(others, others, list_recv.at[0]).wait()
     to_smem = pltpu.make_async_copy(lists, lists_smem, load_sem.at[5])
     to_smem.start()
 
@@ -157,17 +155,19 @@
                 extra = jnp.where(place == 2 * q + half, diagonal[:, lanes], extra)
         send_slots[slot, SLOT_ROWS - 16 : SLOT_ROWS, :] = extra.astype(jnp.bfloat16)
 
-    hops = []
+    parts = [pl.ds(BLOCK * HALF // LANES, SLOT_ROWS - BLOCK * HALF // LANES), pl.ds(0, BLOCK * HALF // LANES)]
+    hops = [[], []]
     for k, (displacement, first, second) in enumerate(RELAYED):
         pack(displacement)
-        copy = pltpu.make_async_remote_copy(
-            src_ref=send_slots.at[SLOT[displacement]], dst_ref=relay_slots.at[k],
-            send_sem=hop_send.at[k], recv_sem=hop_recv.at[k], device_id=(d, at(first)), device_id_type=MESH,
-        )
-        copy.start()
-        hops.append(copy)
+        for p, part in enumerate(parts):
+            copy = pltpu.make_async_remote_copy(
+                src_ref=send_slots.at[SLOT[displacement], part], dst_ref=relay_slots.at[k, part],
+                send_sem=hop_send.at[p, k], recv_sem=hop_recv.at[p, k], device_id=(d, at(first)), device_id_type=MESH,
+            )
+            copy.start()
+            hops[p].append(copy)
     sends = []
-    for displacement in FAR + DIAGONAL + STRAIGHT + NEAR:
+    for displacement in NEAR + STRAIGHT + DIAGONAL + FAR:
         pack(displacement)
         slot = SLOT[displacement]
         copy = pltpu.make_async_remote_copy(
@@ -178,15 +178,16 @@
         sends.append(copy)
     pack((0, 0))
     pltpu.make_async_copy(send_slots.at[0], slots.at[0], slot_recv.at[0]).start()
-    for k, (displacement, first, second) in enumerate(RELAYED):
-        hops[k].wait_recv()
-        slot = SLOT[displacement]
-        copy = pltpu.make_async_remote_copy(
-            src_ref=relay_slots.at[k], dst_ref=slots.at[slot],
-            send_sem=slot_send.at[slot], recv_sem=slot_recv.at[slot], device_id=(d, at(second)), device_id_type=MESH,
-        )
-        copy.start()
-        sends.append(copy)
+    for p, part in enumerate(parts):
+        for k, (displacement, first, second) in enumerate(RELAYED):
+            hops[p][k].wait_recv()
+            slot = SLOT[displacement]
+            copy = pltpu.make_async_remote_copy(
+                src_ref=relay_slots.at[k, part], dst_ref=slots.at[slot, part],
+                send_sem=last_send.at[p, k], recv_sem=last_recv.at[p, k], device_id=(d, at(second)), device_id_type=MESH,
+            )
+            copy.start()
+            sends.append(copy)
 
     for load in own_loads:
         load.wait()
@@ -229,11 +230,13 @@
     def out_copy(slot):
         return pltpu.make_async_copy(slots.at[slot, pl.ds(0, 4 * BLOCK)], scaled_out.at[slot], out_sem.at[slot])
 
-    def slot_step(slot, carry):
-        pltpu.make_async_copy(send_slots.at[slot], slots.at[slot], slot_recv.at[slot]).wait()
+    def apply_right(slot):
+        unpack(slot, 1, right_full)
+        block = blocks[block_of_slot[slot]]
+        return jnp.dot(block, right_full[...], preferred_element_type=jnp.float32).astype(jnp.bfloat16)
+
+    def finish(slot, right_applied):
         j = block_of_slot[slot]
-        unpack(slot, 1, right_full)
-        right_applied = jnp.dot(blocks[j], right_full[...], preferred_element_type=jnp.float32).astype(jnp.bfloat16)
         unpack(slot, 0, left_full)
         preconditioned = jnp.dot(left_full[...], right_applied, preferred_element_type=jnp.float32)
         count = BLOCK * BLOCK
@@ -243,10 +246,29 @@
         for k in range(BLOCK // LANES):
             slots[slot, k * BLOCK : (k + 1) * BLOCK, :] = scaled[:, k * LANES : (k + 1) * LANES]
         out_copy(slot).start()
+
+    def direct_step(slot, carry):
+        pltpu.make_async_copy(send_slots.at[slot], slots.at[slot], slot_recv.at[slot]).wait()
+        finish(slot, apply_right(slot))
         return carry
 
-    lax.fori_loop(0, mp_size, slot_step, 0)
-    for hop in hops:
+    def right_step(k, carry):
+        part = parts[0]
+        pltpu.make_async_copy(send_slots.at[k, part], relay_slots.at[k, part], last_recv.at[0, k]).wait()
+        halfway[k] = apply_right(k + DIRECT)
+        return carry
+
+    def left_step(k, carry):
+        part = parts[1]
+        pltpu.make_async_copy(send_slots.at[k, part], relay_slots.at[k, part], last_recv.at[1, k]).wait()
+        finish(k + DIRECT, halfway[k])
+        return carry
+
+    lax.fori_loop(0, DIRECT, direct_step, 0)
+    lax.fori_loop(0, len(RELAYED), right_step, 0)
+    lax.fori_loop(0, len(RELAYED), left_step, 0)
+    pltpu.make_async_copy(others, others, list_send.at[0]).wait()
+    for hop in hops[0] + hops[1]:
         hop.wait_send()
     for send in sends:
         send.wait_send()
@@ -312,19 +334,22 @@
             full,
             full,
             pltpu.VMEM((4, HALF, HALF), jnp.bfloat16),
-            pltpu.VMEM((8, LANES), jnp.int32),
-            pltpu.VMEM((mp_size, 8, LANES), jnp.int32),
-            pltpu.SMEM((mp_size, 8, LANES), jnp.int32),
+            pltpu.VMEM((len(RELAYED), BLOCK, BLOCK), jnp.bfloat16),
+            pltpu.VMEM((1, LANES), jnp.int32),
+            pltpu.VMEM((mp_size, 1, LANES), jnp.int32),
+            pltpu.SMEM((mp_size, 1, LANES), jnp.int32),
             pltpu.SMEM((mp_size,), jnp.int32),
             pltpu.SMEM((mp_size,), jnp.int32),
             pltpu.SMEM((block_count,), jnp.float32),
             pltpu.SemaphoreType.DMA((6,)),
+            pltpu.SemaphoreType.DMA((1,)),
+            pltpu.SemaphoreType.DMA((1,)),
             pltpu.SemaphoreType.DMA((mp_size,)),
             pltpu.SemaphoreType.DMA((mp_size,)),
-            pltpu.SemaphoreType.DMA((mp_size,)),
-            pltpu.SemaphoreType.DMA((mp_size,)),
-            pltpu.SemaphoreType.DMA((len(RELAYED),)),
-            pltpu.SemaphoreType.DMA((len(RELAYED),)),
+            pltpu.SemaphoreType.DMA((2, len(RELAYED))),
+            pltpu.SemaphoreType.DMA((2, len(RELAYED))),
+            pltpu.SemaphoreType.DMA((2, len(RELAYED))),
+            pltpu.SemaphoreType.DMA((2, len(RELAYED))),
             pltpu.SemaphoreType.DMA((2, dp_size)),
             pltpu.SemaphoreType.DMA((2, dp_size)),
             pltpu.SemaphoreType.DMA((mp_size,)),

time: 118 us -> 115 us (0.975)
  Pallas kernels: 118 us -> 115 us
    pallas_call x1, Pallas kernels: 114 us -> 111 us  [body(): pl.pallas_call(functools.partial(exchange_kernel, rows, columns, dp_size,...]
where the time goes in v3:
time: 115 us
  Pallas kernels  115 us (100%)
    pallas_call x1, Pallas kernels, body(): pl.pallas_call(functools.partial(exchange_kernel, rows, columns, dp_size,...  111 us
    pallas_call x1, Pallas kernels, body(): pl.pallas_call(place_kernel, out_shape=jax.ShapeDtypeStruct((rows, column...  3.76 us

profile of v3, /device:TPU:0, one launch (start us, length us, event | category | flops | bytes accessed | tf_op | source)
XLA Modules:
  0.0 114.8 jit_solution(1680131330950755317)
XLA Ops:
  0.0 111.1 %exchange.1.scaled = bf16[16,2048,128]{2,1,0:T(8,128)(2,1)} custom-call(s32[2,3]{1,0:T(2,128)} %owner.3, bf16[12,512,512]{2,1,0:T(8,128)(2,1)} %left_hbm.1, bf16[12,512,512]{2,1,0:T(8,128)(2,1)} %right_hbm.1, bf16[4,128,8192]{2,1,0:T(8,128)(2,1)} %hidden_hbm.1, bf16[128,1536]{1,0:T(8,128)(2,1)} %grads_hbm.1, s32[512,1536]{1,0:T(8,128)} %words_hbm.1), custom_call_target="tpu_custom_call" | custom-call | tf_op jit(solution)/shard_map/exchange/pallas_call | solution.py:318
  111.1 3.8 %place.1 = bf16[1024,1536]{1,0:T(8,128)(2,1)} custom-call(s32[2,3]{1,0:T(2,128)} %owner.3, bf16[16,2048,128]{2,1,0:T(8,128)(2,1)} %exchange.1.scaled), custom_call_target="tpu_custom_call" | custom-call | tf_op jit(solution)/shard_map/place/pallas_call | solution.py:362

commit v4 on v3

--- a/solution.py
+++ b/solution.py
@@ -27,6 +27,10 @@
 ORDER = [(0, 0)] + NEAR + STRAIGHT + DIAGONAL + FAR + [legs[0] for legs in RELAYED]
 DIRECT = len(ORDER) - len(RELAYED)
 SLOT = {displacement: slot for slot, displacement in enumerate(ORDER)}
+SLOT_CODES = [
+    (sum(SLOT[away % SIDE, away // SIDE] << (4 * (away - low)) for away in range(low, low + 8)) + 2**31) % 2**32 - 2**31
+    for low in (0, 8)
+]
 
 KEPT_ROWS = sum(bits << (4 * code) for code, bits in enumerate((3, 5, 9, 6, 10, 12)))
 
@@ -44,13 +48,14 @@
     rows, columns, dp_size, mp_size,
     owner, left_hbm, right_hbm, hidden_hbm, grads_hbm, words_hbm,
     scaled_out,
-    left, right, send_slots, relay_slots, slots, hidden, grads, words, blocks, kept, left_full, right_full, triangles, halfway,
+    left, right, send_slots, relay_slots, slots, hidden, grads, words, left_full, right_full, triangles,
     tile, lists, lists_smem, ranks, block_of_slot, norms,
-    load_sem, list_send, list_recv, slot_send, slot_recv, hop_send, hop_recv, last_send, last_recv, gather_send, gather_recv, out_sem,
+    load_sem, list_send, list_recv, slot_send, slot_recv, hop_send, hop_recv, last_send, last_recv, gather_send, gather_recv,
 ):
     capacity = left.shape[0]
     down, across = owner.shape
     block_count = down * across
+    blocks, kept, halfway = left.at[pl.ds(0, block_count)], left.at[pl.ds(block_count, block_count)], right
     d, m = lax.axis_index("dp"), lax.axis_index("mp")
     x, y = lax.rem(m, SIDE), m // SIDE
 
@@ -227,9 +232,6 @@
             mixed * triangles[1] + turned * triangles[2] + triangles[3] * diagonal.astype(jnp.bfloat16)
         )
 
-    def out_copy(slot):
-        return pltpu.make_async_copy(slots.at[slot, pl.ds(0, 4 * BLOCK)], scaled_out.at[slot], out_sem.at[slot])
-
     def apply_right(slot):
         unpack(slot, 1, right_full)
         block = blocks[block_of_slot[slot]]
@@ -243,9 +245,7 @@
         numerator = jnp.sqrt(norms[j] / count)
         denominator = jnp.sqrt(jnp.sum(preconditioned * preconditioned) / count + 1e-06)
         scaled = (preconditioned * (numerator / denominator)).astype(jnp.bfloat16) * kept[j]
-        for k in range(BLOCK // LANES):
-            slots[slot, k * BLOCK : (k + 1) * BLOCK, :] = scaled[:, k * LANES : (k + 1) * LANES]
-        out_copy(slot).start()
+        scaled_out[slot] = scaled
 
     def direct_step(slot, carry):
         pltpu.make_async_copy(send_slots.at[slot], slots.at[slot], slot_recv.at[slot]).wait()
@@ -272,38 +272,27 @@
         hop.wait_send()
     for send in sends:
         send.wait_send()
-    for slot in range(mp_size):
-        out_copy(slot).wait()
-
-
-def place_kernel(owner, scaled, out, held, load_sem, store_sem):
+
+
+def place_kernel(owner, scaled, out, sem):
     down, across = owner.shape
     m = lax.axis_index("mp")
-    loads, stores = [], []
+    copies = []
     for j in range(down * across):
         target = owner[j // across, j % across]
         away_x = lax.rem(lax.rem(m, SIDE) - lax.rem(target, SIDE) + SIDE, SIDE)
         away_y = lax.rem(m // SIDE - target // SIDE + SIDE, SIDE)
-        slot = jnp.int32(0)
-        for index, (dx, dy) in enumerate(ORDER):
-            slot = jnp.where((away_x == dx) & (away_y == dy), jnp.int32(index), slot)
+        away = away_y * SIDE + away_x
+        slot = lax.rem(away, 8) * 4
+        slot = jnp.bitwise_and(jnp.where(
+            away < 8, lax.shift_right_logical(jnp.int32(SLOT_CODES[0]), slot), lax.shift_right_logical(jnp.int32(SLOT_CODES[1]), slot)
+        ), 15)
         rows = pl.ds(j // across * BLOCK, BLOCK)
         columns = pl.ds(j % across * BLOCK, BLOCK)
-        loads.append([
-            pltpu.make_async_copy(
-                scaled.at[slot, pl.ds(k * BLOCK, BLOCK)], held.at[j, :, pl.ds(k * LANES, LANES)], load_sem.at[j, k]
-            )
-            for k in range(BLOCK // LANES)
-        ])
-        stores.append(pltpu.make_async_copy(held.at[j], out.at[rows, columns], store_sem.at[j]))
-        for load in loads[-1]:
-            load.start()
-    for parts, store in zip(loads, stores):
-        for load in parts:
-            load.wait()
-        store.start()
-    for store in stores:
-        store.wait()
+        copies.append(pltpu.make_async_copy(scaled.at[slot], out.at[rows, columns], sem.at[j]))
+        copies[-1].start()
+    for copy in copies:
+        copy.wait()
 
 
 def body(dp_size, mp_size, hidden, out_grads, mask_words, owner, left_root, right_root):
@@ -311,15 +300,16 @@
     rows = hidden.shape[2] // dp_size
     block_count = owner.size
     any_space = pl.BlockSpec(memory_space=pl.ANY)
+    in_hbm = pl.BlockSpec(memory_space=pltpu.HBM)
     in_smem = pl.BlockSpec(memory_space=pltpu.SMEM)
     blocks = pltpu.VMEM((block_count, BLOCK, BLOCK), jnp.bfloat16)
     slots = pltpu.VMEM((mp_size, SLOT_ROWS, LANES), jnp.bfloat16)
     full = pltpu.VMEM((BLOCK, BLOCK), jnp.bfloat16)
     scaled = pl.pallas_call(
         functools.partial(exchange_kernel, rows, columns, dp_size, mp_size),
-        out_shape=jax.ShapeDtypeStruct((mp_size, 4 * BLOCK, LANES), jnp.bfloat16),
-        in_specs=[in_smem] + [any_space] * 5,
-        out_specs=any_space,
+        out_shape=pltpu.VMEM((mp_size, BLOCK, BLOCK), jnp.bfloat16),
+        in_specs=[in_smem] + [in_hbm] * 5,
+        out_specs=pl.BlockSpec(memory_space=pltpu.VMEM),
         scratch_shapes=[
             pltpu.VMEM(left_root.shape, jnp.bfloat16),
             pltpu.VMEM(right_root.shape, jnp.bfloat16),
@@ -329,12 +319,9 @@
             pltpu.VMEM((dp_size, tokens, rows), jnp.bfloat16),
             pltpu.VMEM((dp_size, tokens, columns), jnp.bfloat16),
             pltpu.VMEM((rows // 16, columns), jnp.int32),
-            blocks,
-            blocks,
             full,
             full,
             pltpu.VMEM((4, HALF, HALF), jnp.bfloat16),
-            pltpu.VMEM((len(RELAYED), BLOCK, BLOCK), jnp.bfloat16),
             pltpu.VMEM((1, LANES), jnp.int32),
             pltpu.VMEM((mp_size, 1, LANES), jnp.int32),
             pltpu.SMEM((mp_size, 1, LANES), jnp.int32),
@@ -352,10 +339,9 @@
             pltpu.SemaphoreType.DMA((2, len(RELAYED))),
             pltpu.SemaphoreType.DMA((2, dp_size)),
             pltpu.SemaphoreType.DMA((2, dp_size)),
-            pltpu.SemaphoreType.DMA((mp_size,)),
         ],
         compiler_params=pltpu.CompilerParams(
-            collective_id=0, has_side_effects=True, vmem_limit_bytes=58 * 2**20
+            collective_id=0, has_side_effects=True, vmem_limit_bytes=58458112
         ),
         name="exchange",
     )(owner, left_root, right_root, hidden, out_grads, mask_words)
@@ -365,10 +351,9 @@
         in_specs=[in_smem, any_space],
         out_specs=any_space,
         scratch_shapes=[
-            blocks,
-            pltpu.SemaphoreType.DMA((block_count, BLOCK // LANES)),
             pltpu.SemaphoreType.DMA((block_count,)),
         ],
+        compiler_params=pltpu.CompilerParams(vmem_limit_bytes=2**20),
         name="place",
     )(owner, scaled)
 

time: 115 us -> 113 us (0.983)
  Pallas kernels: 115 us -> 113 us
    pallas_call x1, Pallas kernels: 3.76 us -> 2.29 us  [body(): pl.pallas_call(place_kernel, out_shape=jax.ShapeDtypeStruct((rows, column...]
where the time goes in v4:
time: 113 us
  Pallas kernels  113 us (100%)
    pallas_call x1, Pallas kernels, body(): pl.pallas_call(functools.partial(exchange_kernel, rows, columns, dp_size,...  110 us
    pallas_call x1, Pallas kernels, body(): pl.pallas_call(place_kernel, out_shape=jax.ShapeDtypeStruct((rows, column...  2.29 us

profile of v4, /device:TPU:0, one launch (start us, length us, event | category | flops | bytes accessed | tf_op | source)
XLA Modules:
  0.0 112.5 jit_solution(16195744409273634927)
XLA Ops:
  0.0 0.0 copy-start
  0.0 110.2 %exchange.1.scaled = bf16[16,512,512]{2,1,0:T(8,128)(2,1)S(1)} custom-call(s32[2,3]{1,0:T(2,128)} %owner.3, bf16[12,512,512]{2,1,0:T(8,128)(2,1)} %left_hbm.1, bf16[12,512,512]{2,1,0:T(8,128)(2,1)} %right_hbm.1, bf16[4,128,8192]{2,1,0:T(8,128)(2,1)} %hidden_hbm.1, bf16[128,1536]{1,0:T(8,128)(2,1)} %grads_hbm.1, s32[512,1536]{1,0:T(8,128)} %words_hbm.1), custom_call_target="tpu_custom_call" | custom-call | tf_op jit(solution)/shard_map/exchange/pallas_call | solution.py:308
  110.2 0.0 copy-done
  110.2 2.3 %place.1 = bf16[1024,1536]{1,0:T(8,128)(2,1)} custom-call(s32[2,3]{1,0:T(2,128)S(1)} %copy-done, bf16[16,512,512]{2,1,0:T(8,128)(2,1)S(1)} %exchange.1.scaled), custom_call_target="tpu_custom_call" | custom-call | tf_op jit(solution)/shard_map/place/pallas_call | solution.py:348
Async XLA Ops:
  0.0 110.2 %copy-start = (s32[2,3]{1,0:T(2,128)S(1)}, s32[2,3]{1,0:T(2,128)}, u32[]{:S(2)}) copy-start(s32[2,3]{1,0:T(2,128)} %owner.3) | copy-start | bytes 76

commit v5 on v4

--- a/solution.py
+++ b/solution.py
@@ -49,7 +49,7 @@
     owner, left_hbm, right_hbm, hidden_hbm, grads_hbm, words_hbm,
     scaled_out,
     left, right, send_slots, relay_slots, slots, hidden, grads, words, left_full, right_full, triangles,
-    tile, lists, lists_smem, ranks, block_of_slot, norms,
+    tile, lists, ranks, block_of_slot, norms,
     load_sem, list_send, list_recv, slot_send, slot_recv, hop_send, hop_recv, last_send, last_recv, gather_send, gather_recv,
 ):
     capacity = left.shape[0]
@@ -65,6 +65,12 @@
     expert = m * columns // (columns * SIDE)
     own_features = pl.ds(pl.multiple_of(d * rows, rows), rows)
     own_words = pl.ds(pl.multiple_of(d * (rows // 16), rows // 16), rows // 16)
+    barrier = pltpu.get_barrier_semaphore()
+    for step in range(1, mp_size):
+        pl.semaphore_signal(barrier, inc=1, device_id=(d, lax.rem(m + step, mp_size)), device_id_type=MESH)
+    for step in range(1, dp_size):
+        pl.semaphore_signal(barrier, inc=1, device_id=(lax.rem(d + step, dp_size), m), device_id_type=MESH)
+
     root_loads = [
         pltpu.make_async_copy(left_hbm, left, load_sem.at[0]),
         pltpu.make_async_copy(right_hbm, right, load_sem.at[1]),
@@ -77,30 +83,28 @@
     for load in root_loads + own_loads:
         load.start()
 
-    barrier = pltpu.get_barrier_semaphore()
-    for step in range(1, mp_size):
-        pl.semaphore_signal(barrier, inc=1, device_id=(d, lax.rem(m + step, mp_size)), device_id_type=MESH)
-    for step in range(1, dp_size):
-        pl.semaphore_signal(barrier, inc=1, device_id=(lax.rem(d + step, dp_size), m), device_id_type=MESH)
-
     targets = [owner[j // across, j % across] for j in range(block_count)]
-    lane = lax.broadcasted_iota(jnp.int32, (1, LANES), 1)
-    listed = jnp.full((1, LANES), -1, jnp.int32)
     for j in range(block_count):
-        listed = jnp.where(lane == j, targets[j], listed)
-    tile[...] = listed
+        tile[0, j] = targets[j]
+
+    def clear(j, carry):
+        tile[0, j] = jnp.int32(-1)
+        return carry
+
+    lax.fori_loop(block_count, LANES, clear, 0)
     row = lax.broadcasted_iota(jnp.int32, (HALF, HALF), 0)
     column = lax.broadcasted_iota(jnp.int32, (HALF, HALF), 1)
     for k, test in enumerate((row >= column, row < column, row > column, row == column)):
         triangles[k] = jnp.where(test, 1.0, 0.0).astype(jnp.bfloat16)
     pl.semaphore_wait(barrier, mp_size - 1 + dp_size - 1)
 
-    for step in range(1, mp_size):
+    for displacement in FAR + [legs[0] for legs in RELAYED] + DIAGONAL + STRAIGHT + NEAR:
         pltpu.make_async_remote_copy(
             src_ref=tile, dst_ref=lists.at[m], send_sem=list_send.at[0], recv_sem=list_recv.at[0],
-            device_id=(d, lax.rem(m + step, mp_size)), device_id_type=MESH,
+            device_id=(d, at(displacement)), device_id_type=MESH,
         ).start()
-    lists[m] = listed
+    for j in range(block_count):
+        lists[m, 0, j] = targets[j]
 
     gathers = []
     for step in range(1, dp_size):
@@ -119,52 +123,51 @@
 
     others = lists.at[pl.ds(0, mp_size - 1)]
     pltpu.make_async_copy(others, others, list_recv.at[0]).wait()
-    to_smem = pltpu.make_async_copy(lists, lists_smem, load_sem.at[5])
-    to_smem.start()
-
     for slot, displacement in enumerate(ORDER):
         sender = at((SIDE - displacement[0], SIDE - displacement[1]))
         block = jnp.int32(0)
         for j in range(1, block_count):
             block = jnp.where(targets[j] == sender, jnp.int32(j), block)
         block_of_slot[slot] = block
-    to_smem.wait()
 
     def rank_step(sender, taken):
         ranks[sender] = jnp.minimum(taken, capacity - 1)
         hit = jnp.int32(0)
         for j in range(block_count):
-            hit = jnp.where(lists_smem[sender, 0, j] == m, jnp.int32(1), hit)
+            hit = jnp.where(lists[sender, 0, j] == m, jnp.int32(1), hit)
         return taken + hit
 
     lax.fori_loop(0, mp_size, rank_step, jnp.int32(0))
     for load in root_loads:
         load.wait()
 
-    def pack(displacement):
+    def pack(displacement, halves=(1, 0)):
         slot = SLOT[displacement]
         rank = ranks[at(displacement)]
-        place = lax.broadcasted_iota(jnp.int32, (16, LANES), 0)
-        extra = jnp.zeros((16, LANES), jnp.float32)
-        for q, root in enumerate((left, right)):
-            a = root[rank, 0:HALF, 0:HALF]
+        for q in halves:
+            root = (left, right)[q]
             b = root[rank, 0:HALF, HALF:BLOCK]
-            c = root[rank, HALF:BLOCK, HALF:BLOCK]
-            mixed = a * triangles[0] + c * triangles[1]
-            diagonal = jnp.sum((c * triangles[3]).astype(jnp.float32), axis=0, keepdims=True)
+            mixed = root[rank, 0:HALF, 0:HALF] * triangles[0] + root[rank, HALF:BLOCK, HALF:BLOCK] * triangles[1]
             base = q * 4 * HALF
             for half in range(2):
                 lanes = slice(half * LANES, (half + 1) * LANES)
                 send_slots[slot, base + half * HALF : base + (half + 1) * HALF, :] = b[:, lanes]
                 send_slots[slot, base + (2 + half) * HALF : base + (3 + half) * HALF, :] = mixed[:, lanes]
-                extra = jnp.where(place == 2 * q + half, diagonal[:, lanes], extra)
-        send_slots[slot, SLOT_ROWS - 16 : SLOT_ROWS, :] = extra.astype(jnp.bfloat16)
+        if 1 in halves:
+            place = lax.broadcasted_iota(jnp.int32, (16, LANES), 0)
+            extra = jnp.zeros((16, LANES), jnp.float32)
+            for q, root in enumerate((left, right)):
+                last = (root[rank, HALF:BLOCK, HALF:BLOCK] * triangles[3]).astype(jnp.float32)
+                diagonal = jnp.sum(last, axis=0, keepdims=True)
+                for half in range(2):
+                    extra = jnp.where(place == 2 * q + half, diagonal[:, half * LANES : (half + 1) * LANES], extra)
+            send_slots[slot, SLOT_ROWS - 16 : SLOT_ROWS, :] = extra.astype(jnp.bfloat16)
 
     parts = [pl.ds(BLOCK * HALF // LANES, SLOT_ROWS - BLOCK * HALF // LANES), pl.ds(0, BLOCK * HALF // LANES)]
     hops = [[], []]
-    for k, (displacement, first, second) in enumerate(RELAYED):
-        pack(displacement)
-        for p, part in enumerate(parts):
+    for p, part in enumerate(parts):
+        for k, (displacement, first, second) in enumerate(RELAYED):
+            pack(displacement, (1 - p,))
             copy = pltpu.make_async_remote_copy(
                 src_ref=send_slots.at[SLOT[displacement], part], dst_ref=relay_slots.at[k, part],
                 send_sem=hop_send.at[p, k], recv_sem=hop_recv.at[p, k], device_id=(d, at(first)), device_id_type=MESH,
@@ -322,8 +325,7 @@
             full,
             full,
             pltpu.VMEM((4, HALF, HALF), jnp.bfloat16),
-            pltpu.VMEM((1, LANES), jnp.int32),
-            pltpu.VMEM((mp_size, 1, LANES), jnp.int32),
+            pltpu.SMEM((1, LANES), jnp.int32),
             pltpu.SMEM((mp_size, 1, LANES), jnp.int32),
             pltpu.SMEM((mp_size,), jnp.int32),
             pltpu.SMEM((mp_size,), jnp.int32),

time: 113 us -> 111 us (0.982)
  Pallas kernels: 113 us -> 111 us
    pallas_call x1, Pallas kernels: 110 us -> 109 us  [body(): pl.pallas_call(functools.partial(exchange_kernel, rows, columns, dp_size,...]
where the time goes in v5:
time: 111 us
  Pallas kernels  111 us (100%)
    pallas_call x1, Pallas kernels, body(): pl.pallas_call(functools.partial(exchange_kernel, rows, columns, dp_size,...  109 us
    pallas_call x1, Pallas kernels, body(): pl.pallas_call(place_kernel, out_shape=jax.ShapeDtypeStruct((rows, column...  2.29 us

profile of v5, /device:TPU:0, one launch (start us, length us, event | category | flops | bytes accessed | tf_op | source)
XLA Modules:
  0.0 111.4 jit_solution(14135575003058281404)
XLA Ops:
  0.0 0.0 copy-start
  0.0 109.1 %exchange.1.scaled = bf16[16,512,512]{2,1,0:T(8,128)(2,1)S(1)} custom-call(s32[2,3]{1,0:T(2,128)} %owner.3, bf16[12,512,512]{2,1,0:T(8,128)(2,1)} %left_hbm.1, bf16[12,512,512]{2,1,0:T(8,128)(2,1)} %right_hbm.1, bf16[4,128,8192]{2,1,0:T(8,128)(2,1)} %hidden_hbm.1, bf16[128,1536]{1,0:T(8,128)(2,1)} %grads_hbm.1, s32[512,1536]{1,0:T(8,128)} %words_hbm.1), custom_call_target="tpu_custom_call" | custom-call | tf_op jit(solution)/shard_map/exchange/pallas_call | solution.py:311
  109.1 0.0 copy-done
  109.1 2.3 %place.1 = bf16[1024,1536]{1,0:T(8,128)(2,1)} custom-call(s32[2,3]{1,0:T(2,128)S(1)} %copy-done, bf16[16,512,512]{2,1,0:T(8,128)(2,1)S(1)} %exchange.1.scaled), custom_call_target="tpu_custom_call" | custom-call | tf_op jit(solution)/shard_map/place/pallas_call | solution.py:350
Async XLA Ops:
  0.0 109.1 %copy-start = (s32[2,3]{1,0:T(2,128)S(1)}, s32[2,3]{1,0:T(2,128)}, u32[]{:S(2)}) copy-start(s32[2,3]{1,0:T(2,128)} %owner.3) | copy-start | bytes 76

commit v6 on v5

--- a/solution.py
+++ b/solution.py
@@ -24,7 +24,7 @@
     ((2, 3), (0, 3), (2, 0)),
     ((3, 2), (3, 0), (0, 2)),
 ]
-ORDER = [(0, 0)] + NEAR + STRAIGHT + DIAGONAL + FAR + [legs[0] for legs in RELAYED]
+ORDER = [(0, 0)] + NEAR + DIAGONAL + FAR + STRAIGHT + [legs[0] for legs in RELAYED]
 DIRECT = len(ORDER) - len(RELAYED)
 SLOT = {displacement: slot for slot, displacement in enumerate(ORDER)}
 SLOT_CODES = [
@@ -175,7 +175,7 @@
             copy.start()
             hops[p].append(copy)
     sends = []
-    for displacement in NEAR + STRAIGHT + DIAGONAL + FAR:
+    for displacement in NEAR + DIAGONAL + FAR + STRAIGHT:
         pack(displacement)
         slot = SLOT[displacement]
         copy = pltpu.make_async_remote_copy(
@@ -186,6 +186,7 @@
         sends.append(copy)
     pack((0, 0))
     pltpu.make_async_copy(send_slots.at[0], slots.at[0], slot_recv.at[0]).start()
+    forwards = []
     for p, part in enumerate(parts):
         for k, (displacement, first, second) in enumerate(RELAYED):
             hops[p][k].wait_recv()
@@ -195,7 +196,7 @@
                 send_sem=last_send.at[p, k], recv_sem=last_recv.at[p, k], device_id=(d, at(second)), device_id_type=MESH,
             )
             copy.start()
-            sends.append(copy)
+            forwards.append(copy)
 
     for load in own_loads:
         load.wait()
@@ -240,15 +241,16 @@
         block = blocks[block_of_slot[slot]]
         return jnp.dot(block, right_full[...], preferred_element_type=jnp.float32).astype(jnp.bfloat16)
 
-    def finish(slot, right_applied):
+    def scale(slot, preconditioned):
         j = block_of_slot[slot]
-        unpack(slot, 0, left_full)
-        preconditioned = jnp.dot(left_full[...], right_applied, preferred_element_type=jnp.float32)
         count = BLOCK * BLOCK
         numerator = jnp.sqrt(norms[j] / count)
         denominator = jnp.sqrt(jnp.sum(preconditioned * preconditioned) / count + 1e-06)
-        scaled = (preconditioned * (numerator / denominator)).astype(jnp.bfloat16) * kept[j]
-        scaled_out[slot] = scaled
+        scaled_out[slot] = (preconditioned * (numerator / denominator)).astype(jnp.bfloat16) * kept[j]
+
+    def finish(slot, right_applied):
+        unpack(slot, 0, left_full)
+        scale(slot, jnp.dot(left_full[...], right_applied, preferred_element_type=jnp.float32))
 
     def direct_step(slot, carry):
         pltpu.make_async_copy(send_slots.at[slot], slots.at[slot], slot_recv.at[slot]).wait()
@@ -261,20 +263,25 @@
         halfway[k] = apply_right(k + DIRECT)
         return carry
 
-    def left_step(k, carry):
+    def left_step(pair, carry):
         part = parts[1]
-        pltpu.make_async_copy(send_slots.at[k, part], relay_slots.at[k, part], last_recv.at[1, k]).wait()
-        finish(k + DIRECT, halfway[k])
+        both = ((2 * pair, left_full), (2 * pair + 1, right_full))
+        for k, full in both:
+            pltpu.make_async_copy(send_slots.at[k, part], relay_slots.at[k, part], last_recv.at[1, k]).wait()
+            unpack(k + DIRECT, 0, full)
+        products = [jnp.dot(full[...], halfway[k], preferred_element_type=jnp.float32) for k, full in both]
+        for (k, _), product in zip(both, products):
+            scale(k + DIRECT, product)
         return carry
 
     lax.fori_loop(0, DIRECT, direct_step, 0)
     lax.fori_loop(0, len(RELAYED), right_step, 0)
-    lax.fori_loop(0, len(RELAYED), left_step, 0)
     pltpu.make_async_copy(others, others, list_send.at[0]).wait()
-    for hop in hops[0] + hops[1]:
-        hop.wait_send()
-    for send in sends:
-        send.wait_send()
+    for copy in hops[0] + hops[1] + sends:
+        copy.wait_send()
+    lax.fori_loop(0, len(RELAYED) // 2, left_step, 0)
+    for copy in forwards:
+        copy.wait_send()
 
 
 def place_kernel(owner, scaled, out, sem):

time: 111 us -> 111 us (level)
  no operation moved by 1% of the time
where the time goes in v6:
time: 111 us
  Pallas kernels  111 us (100%)
    pallas_call x1, Pallas kernels, body(): pl.pallas_call(functools.partial(exchange_kernel, rows, columns, dp_size,...  108 us
    pallas_call x1, Pallas kernels, body(): pl.pallas_call(place_kernel, out_shape=jax.ShapeDtypeStruct((rows, column...  2.29 us

profile of v6, /device:TPU:0, one launch (start us, length us, event | category | flops | bytes accessed | tf_op | source)
XLA Modules:
  0.0 110.7 jit_solution(15893243776288586808)
XLA Ops:
  0.0 0.0 copy-start
  0.0 108.4 %exchange.1.scaled = bf16[16,512,512]{2,1,0:T(8,128)(2,1)S(1)} custom-call(s32[2,3]{1,0:T(2,128)} %owner.3, bf16[12,512,512]{2,1,0:T(8,128)(2,1)} %left_hbm.1, bf16[12,512,512]{2,1,0:T(8,128)(2,1)} %right_hbm.1, bf16[4,128,8192]{2,1,0:T(8,128)(2,1)} %hidden_hbm.1, bf16[128,1536]{1,0:T(8,128)(2,1)} %grads_hbm.1, s32[512,1536]{1,0:T(8,128)} %words_hbm.1), custom_call_target="tpu_custom_call" | custom-call | tf_op jit(solution)/shard_map/exchange/pallas_call | solution.py:318
  108.4 0.0 copy-done
  108.4 2.3 %place.1 = bf16[1024,1536]{1,0:T(8,128)(2,1)} custom-call(s32[2,3]{1,0:T(2,128)S(1)} %copy-done, bf16[16,512,512]{2,1,0:T(8,128)(2,1)S(1)} %exchange.1.scaled), custom_call_target="tpu_custom_call" | custom-call | tf_op jit(solution)/shard_map/place/pallas_call | solution.py:357
Async XLA Ops:
  0.0 108.4 %copy-start = (s32[2,3]{1,0:T(2,128)S(1)}, s32[2,3]{1,0:T(2,128)}, u32[]{:S(2)}) copy-start(s32[2,3]{1,0:T(2,128)} %owner.3) | copy-start | bytes 76

commit v7 on v6

--- a/solution.py
+++ b/solution.py
@@ -266,10 +266,11 @@
     def left_step(pair, carry):
         part = parts[1]
         both = ((2 * pair, left_full), (2 * pair + 1, right_full))
+        products = []
         for k, full in both:
             pltpu.make_async_copy(send_slots.at[k, part], relay_slots.at[k, part], last_recv.at[1, k]).wait()
             unpack(k + DIRECT, 0, full)
-        products = [jnp.dot(full[...], halfway[k], preferred_element_type=jnp.float32) for k, full in both]
+            products.append(jnp.dot(full[...], halfway[k], preferred_element_type=jnp.float32))
         for (k, _), product in zip(both, products):
             scale(k + DIRECT, product)
         return carry

time: 111 us -> 111 us (level)
  no operation moved by 1% of the time
where the time goes in v7:
time: 111 us
  Pallas kernels  111 us (100%)
    pallas_call x1, Pallas kernels, body(): pl.pallas_call(functools.partial(exchange_kernel, rows, columns, dp_size,...  109 us
    pallas_call x1, Pallas kernels, body(): pl.pallas_call(place_kernel, out_shape=jax.ShapeDtypeStruct((rows, column...  2.29 us

profile of v7, /device:TPU:0, one launch (start us, length us, event | category | flops | bytes accessed | tf_op | source)
XLA Modules:
  0.0 110.9 jit_solution(15114992990828186315)
XLA Ops:
  0.0 0.0 copy-start
  0.0 108.5 %exchange.1.scaled = bf16[16,512,512]{2,1,0:T(8,128)(2,1)S(1)} custom-call(s32[2,3]{1,0:T(2,128)} %owner.3, bf16[12,512,512]{2,1,0:T(8,128)(2,1)} %left_hbm.1, bf16[12,512,512]{2,1,0:T(8,128)(2,1)} %right_hbm.1, bf16[4,128,8192]{2,1,0:T(8,128)(2,1)} %hidden_hbm.1, bf16[128,1536]{1,0:T(8,128)(2,1)} %grads_hbm.1, s32[512,1536]{1,0:T(8,128)} %words_hbm.1), custom_call_target="tpu_custom_call" | custom-call | tf_op jit(solution)/shard_map/exchange/pallas_call | solution.py:319
  108.6 0.0 copy-done
  108.6 2.3 %place.1 = bf16[1024,1536]{1,0:T(8,128)(2,1)} custom-call(s32[2,3]{1,0:T(2,128)S(1)} %copy-done, bf16[16,512,512]{2,1,0:T(8,128)(2,1)S(1)} %exchange.1.scaled), custom_call_target="tpu_custom_call" | custom-call | tf_op jit(solution)/shard_map/place/pallas_call | solution.py:358
Async XLA Ops:
  0.0 108.6 %copy-start = (s32[2,3]{1,0:T(2,128)S(1)}, s32[2,3]{1,0:T(2,128)}, u32[]{:S(2)}) copy-start(s32[2,3]{1,0:T(2,128)} %owner.3) | copy-start | bytes 76
